TPU v7x, 32 devices: a whole 2x2x4 slice. The times are simulated.
32 devices in a mesh: groups: 2 (over x), blk: 16 (over z, y, core).
Axes of the slice: x: 2, y: 2, z: 4, core: 2. Of those that a mesh axis runs over, the one named last changes fastest.
Arguments:
- ocean_state: float32 [2, 6, 256, 3600], P(None, None, ('groups', 'blk')), parts along dimension 2, may hold values from -6 to 6
- kappa_h: float32 [128, 3600], P('blk'), may hold values from 0.02 to 0.15
- kappa_v: float32 [6], replicated, may hold values from 0.02 to 0.15
- wet_depth: int32 [128, 3600], P('blk'), may hold values from 0 to 6
- coupling: float32 [12, 12], replicated, may hold values from -8 to 8
- dest_of_block: int32 [3600, 1], P('blk'), may hold values from 0 to 15; in each aligned block of 225 rows (0 to 224, 225 to 449, ...) at most 22 rows name the same one
- tile_of_block: int32 [3600], P('blk'), may hold values from 0 to 7
- remap_weights: bfloat16 [3600, 128, 128], P('blk'), may hold values from 0.0077819824 to 0.0625
Outputs:
- ocean_next: float32 [2, 6, 256, 3600], P(None, None, ('groups', 'blk')), parts along dimension 2
- atm_fields: float32 [12, 32768], P(None, ('groups', 'blk')), parts along dimension 1
There are 2 independent parts, one for each index of `groups`. A program takes and returns all parts, laid end to end along the dimension named above; an argument that names none is the same for every part. Nothing has to cross between parts.
Inputs may be any that keep to these rules, and one draw needn't show every extreme that they name: `dest_of_block`: among the 225 blocks of one device at most 22 name the same owner, and some owner gets exactly 22 of them.
All inputs are finite; a program needn't handle non-finite values.
Results may differ from a plain program's by a relative error of at most 0.0029.
Values sent between devices are 32-bit elements; how exact they have to be, the bound alone decides.
A program may use at most 64 MiB of HBM per device.

v0:
```python
import jax
import jax.numpy as jnp
from jax import lax
from jax.sharding import PartitionSpec as P

NZ = 6
FIELDS = 12
CB = 128
AT = 128
NTILE = 8


def extended_2(shard, sides, width):
    for axis, dim in sides:
        size, length = (lax.axis_size(axis), shard.shape[dim])
        up = [(i, (i + 1) % size) for i in range(size - 1)]
        down = [(j, i) for i, j in up]
        last = lax.slice_in_dim(shard, length - width, length, axis=dim)
        first = lax.slice_in_dim(shard, 0, width, axis=dim)
        before = lax.ppermute(last, axis, up)
        after = lax.ppermute(first, axis, down)
        shard = jnp.concatenate([before, shard, after], axis=dim)
    return shard


def conductance(kappa_h, wet_depth):
    levels = jnp.arange(NZ, dtype=jnp.int32)[:, None, None]
    return jnp.where(levels < wet_depth[None], kappa_h[None], jnp.zeros_like(kappa_h)[None])


def mix_step(extended, conduct, kappa_v):
    centre = extended[:, :, 1:-1]
    conduct_mid = conduct[:, 1:-1]
    east_face = jnp.sqrt(conduct_mid * jnp.roll(conduct_mid, -1, axis=-1))
    east_flux = east_face * (jnp.roll(centre, -1, axis=-1) - centre)
    change = east_flux - jnp.roll(east_flux, 1, axis=-1)
    north_face = jnp.sqrt(conduct[:, 1:] * conduct[:, :-1])
    north_flux = north_face * (extended[:, :, 1:] - extended[:, :, :-1])
    change = change + north_flux[:, :, 1:] - north_flux[:, :, :-1]
    wet_mask = jnp.where(conduct_mid > 0.0, jnp.ones_like(conduct_mid), jnp.zeros_like(conduct_mid))
    vert_coef = kappa_v[:-1, None, None] * wet_mask[:-1] * wet_mask[1:]
    vert_flux = vert_coef * (centre[:, 1:] - centre[:, :-1])
    zero_level = jnp.zeros_like(centre[:, :1])
    change = (
        change
        + jnp.concatenate([vert_flux, zero_level], axis=1)
        - jnp.concatenate([zero_level, vert_flux], axis=1)
    )
    return centre + change


def body(
    ocean_state, kappa_h, kappa_v, wet_depth, coupling, dest_of_block, tile_of_block, remap_weights
):
    conduct = conductance(kappa_h, wet_depth)
    stacked = jnp.concatenate([ocean_state, conduct[None]], axis=0)
    extended = extended_2(stacked, (("blk", 2),), 1)
    conduct_ext = extended[2]
    ocean_mid = mix_step(extended[:2], conduct_ext, kappa_v)
    second_ext = extended_2(ocean_mid, (("blk", 2),), 1)
    ocean_next = mix_step(second_ext, conduct_ext, kappa_v)
    band_cells = ocean_next.shape[2] * ocean_next.shape[3]
    profile = ocean_next.reshape(2 * NZ, band_cells)
    fields = jnp.dot(coupling, profile, precision=lax.Precision.HIGHEST)
    sea_mask = jnp.where(wet_depth > 0, jnp.ones_like(kappa_h), jnp.zeros_like(kappa_h)).reshape(-1)
    surface = jnp.concatenate([fields * sea_mask[None], sea_mask[None]], axis=0).astype(
        jnp.bfloat16
    )
    block_count = remap_weights.shape[0]
    blocks = surface.reshape(FIELDS + 1, block_count, CB).transpose(1, 0, 2)
    partial_value = jnp.einsum(
        "brc,bca->bra", blocks, remap_weights, preferred_element_type=jnp.float32
    )
    owner_dev = dest_of_block[:, 0]
    devices = lax.axis_size("blk")
    capacity = max(2, 3 * block_count // (2 * devices) + 1)
    owners = (owner_dev[:, None] == jnp.arange(devices, dtype=jnp.int32)[None]).astype(jnp.int32)
    earlier = jnp.cumsum(owners, axis=0) - owners
    slot_index = jnp.sum(earlier * owners, axis=1)
    position = owner_dev * capacity + slot_index
    buffer = (
        jnp.zeros((devices * capacity, FIELDS + 1, AT), jnp.float32).at[position].set(partial_value)
    )
    labels = (
        jnp.full((devices * capacity,), -1.0, jnp.float32)
        .at[position]
        .set(tile_of_block.astype(jnp.float32))
    )
    arrived, arrived_labels = (
        lax.all_to_all(
            buffer.reshape(devices, capacity, FIELDS + 1, AT),
            "blk",
            split_axis=0,
            concat_axis=0,
            tiled=True,
        ),
        lax.all_to_all(
            labels.reshape(devices, capacity), "blk", split_axis=0, concat_axis=0, tiled=True
        ),
    )
    selector = (
        arrived_labels.reshape(-1)[:, None] == jnp.arange(NTILE, dtype=jnp.float32)[None]
    ).astype(jnp.float32)
    tile_sum = jnp.einsum(
        "st,sk->tk",
        selector,
        arrived.reshape(devices * capacity, (FIELDS + 1) * AT),
        precision=lax.Precision.HIGHEST,
    )
    tile_sum = tile_sum.reshape(NTILE, FIELDS + 1, AT)
    numerator = tile_sum[:, :FIELDS]
    denominator = jnp.maximum(tile_sum[:, FIELDS], 1.0)
    atm_fields = (numerator / denominator[:, None]).transpose(1, 0, 2).reshape(FIELDS, NTILE * AT)
    return (ocean_next, atm_fields)


def solution(mesh):
    return jax.shard_map(
        body,
        mesh=mesh,
        in_specs=(
            P(None, None, ("groups", "blk"), None),
            P("blk", None),
            P(),
            P("blk", None),
            P(),
            P("blk", None),
            P("blk"),
            P("blk", None, None),
        ),
        out_specs=(P(None, None, ("groups", "blk"), None), P(None, ("groups", "blk"))),
        check_vma=False,
    )
```

profile of v0, /device:TPU:13, one launch (start us, length us, event | category | flops | bytes accessed | tf_op | source)
XLA Modules:
  0.0 151.5 jit_solution(14815204469958206296)
XLA Ops:
  0.7 0.7 convert_element_type.11
  1.4 0.7 iota_compare_fusion.1
  3.0 0.7 fusion.24
  3.7 0.7 compare_select_fusion.2
  4.4 1.3 scatter_custom_fusion
  5.7 0.7 all_to_all.9
  6.4 6.6 %all-to-all-start = ((f32[16,1,22]{2,1,0:T(1,128)}), f32[16,1,22]{2,1,0:T(1,128)S(1)}, u32[]{:S(2)}, u32[]{:S(2)}) async-start(f32[16,1,22]{2,1,0:T(1,128)} %all_to_all.9), calls=%async_computation | async-start | bytes 16384 | tf_op jit(solution)/shard_map/all_to_all | solution.py:97
  12.9 1.7 %copy.55 = f32[2,6,8,3600]{3,1,2,0:T(8,128)S(1)} copy(f32[2,6,8,3600]{3,2,1,0:T(8,128)} %param.8) | data formatting | bytes 2764800 | tf_op args[0]
  14.8 0.9 pad_maximum_fusion.7
  15.7 2.3 %collective-permute-start.1 = (f32[3,6,1,3600]{3,1,2,0:T(8,128)}, f32[3,6,1,3600]{3,1,2,0:T(8,128)S(1)}, u32[]{:S(2)}, u32[]{:S(2)}) collective-permute-start(f32[3,6,1,3600]{3,1,2,0:T(8,128)} %get-tuple-element.8), channel_id=1, source_target_pairs={{1,0},{2,1},{3,2},{4,3},{5,4},{6,5},{7,6},{8,7},{9,8},{10,9},{11,1... | collective-permute-start | bytes 777608 | tf_op jit(solution)/shard_map/ppermute | solution.py:21
  18.0 4.2 %collective-permute-start = (f32[3,6,1,3600]{3,1,2,0:T(8,128)}, f32[3,6,1,3600]{3,1,2,0:T(8,128)}, u32[]{:S(2)}, u32[]{:S(2)}) collective-permute-start(f32[3,6,1,3600]{3,1,2,0:T(8,128)} %get-tuple-element.9), channel_id=1, source_target_pairs={{0,1},{1,2},{2,3},{3,4},{4,5},{5,6},{6,7},{7,8},{8,9},{9,10},{10,1... | collective-permute-start | bytes 777608 | tf_op jit(solution)/shard_map/ppermute | solution.py:20
  22.8 1.8 %slice.177 = f32[2,6,8,3599]{3,1,2,0:T(8,128)} slice(f32[2,6,8,3600]{3,1,2,0:T(8,128)S(1)} %copy.55), slice={[0:2], [0:6], [0:8], [1:3600]} | slice | bytes 2764032 | tf_op jit(solution)/shard_map/jit(_roll_static)/slice | solution.py:35
  24.7 0.7 mul.106
  25.4 1.0 concatenate.77
  26.9 1.0 fusion.15
  29.6 1.1 copy-done.1
  31.9 1.2 fusion.3
  33.1 1.0 fusion.12
  34.9 5.3 %collective-permute-start.3 = (f32[2,6,1,3600]{3,1,2,0:T(8,128)S(1)}, f32[2,6,1,3600]{3,1,2,0:T(8,128)S(1)}, u32[]{:S(2)}, u32[]{:S(2)}) collective-permute-start(f32[2,6,1,3600]{3,1,2,0:T(8,128)S(1)} %get-tuple-element.10), channel_id=1, source_target_pairs={{0,1},{1,2},{2,3},{3,4},{4,5},{5,6},{6,7},{7,8},{8,9},{9,10},{10,1... | collective-permute-start | bytes 518408 | tf_op jit(solution)/shard_map/ppermute | solution.py:20
  40.3 2.1 %collective-permute-start.2 = (f32[2,6,1,3600]{3,1,2,0:T(8,128)S(1)}, f32[2,6,1,3600]{3,1,2,0:T(8,128)S(1)}, u32[]{:S(2)}, u32[]{:S(2)}) collective-permute-start(f32[2,6,1,3600]{3,1,2,0:T(8,128)S(1)} %get-tuple-element.11), channel_id=1, source_target_pairs={{1,0},{2,1},{3,2},{4,3},{5,4},{6,5},{7,6},{8,7},{9,8},{10,9},{11,1... | collective-permute-start | bytes 518408 | tf_op jit(solution)/shard_map/ppermute | solution.py:21
  43.3 5.3 %collective-permute-done.2 = f32[2,6,1,3600]{3,1,2,0:T(8,128)S(1)} collective-permute-done((f32[2,6,1,3600]{3,1,2,0:T(8,128)S(1)}, f32[2,6,1,3600]{3,1,2,0:T(8,128)S(1)}, u32[]{:S(2)}, u32[]{:S(2)}) %collective-permute-start.2) | collective-permute-done | bytes 172832 | tf_op jit(solution)/shard_map/ppermute | solution.py:21
  48.9 0.8 fusion.8
  51.0 2.6 %fusion.1 = bf16[12,28800]{1,0:T(8,128)(2,1)} fusion(f32[12,28800]{1,0:T(8,128)S(1)} %reshape.60, f32[12,12]{1,0:T(8,128)S(1)} %copy-done, f32[28800]{0:T(1024)S(1)} %copy-done.5), kind=kOutput, calls=%fused_computation.4 | convolution fusion | flops 50457600 | bytes 2189376 | tf_op jit(solution)/shard_map/dot_general | solution.py:64
  53.6 1.7 %concatenate.74 = bf16[12,225,128]{2,1,0:T(8,128)(2,1)S(1)} reshape(bf16[12,28800]{1,0:T(8,128)(2,1)} %fusion.1) | data formatting | bytes 1382400 | tf_op jit(solution)/shard_map/concatenate | solution.py:66
  55.6 6.4 %fusion.19 = f32[225,13,128]{2,1,0:T(8,128)} fusion(bf16[225,128,128]{2,1,0:T(8,128)(2,1)} %param.15, bf16[1,225,128]{2,0,1:T(2,128)(2,1)S(1)} %concatenate.77, bf16[12,225,128]{2,0,1:T(8,128)(2,1)S(1)} %copy.59), kind=kOutput, calls=%fused_computation.48 | convolution fusion | flops 97344000 | bytes 9619200 | tf_op jit(solution)/shard_map/brc,bca->bra/dot_general | solution.py:71
  62.2 17.6 %scatter_fusion = f32[352,13,128]{2,1,0:T(8,128)S(1)} fusion(f32[352,13,128]{2,1,0:T(8,128)S(1)} %broadcast_in_dim.27, s32[225]{0:T(256)S(1)} %bitcast.64, f32[225,13,128]{2,1,0:T(8,128)} %fusion.19), kind=kCustom, calls=%fused_computation.1 | custom fusion | bytes 4493700 | tf_op jit(solution)/shard_map/scatter | solution.py:82
  79.7 2.2 %copy.62 = f32[16,22,13,128]{3,1,2,0:T(8,128)} copy(f32[16,22,13,128]{3,2,1,0:T(8,128)S(1)} %bitcast.53) | data formatting | bytes 4685824 | tf_op jit(solution)/shard_map/reshape | solution.py:91
  82.0 4.9 %all-to-all-start.1 = ((f32[16,22,13,128]{3,1,2,0:T(8,128)}), f32[16,22,13,128]{3,1,2,0:T(8,128)S(1)}, u32[]{:S(2)}, u32[]{:S(2)}) async-start(f32[16,22,13,128]{3,1,2,0:T(8,128)} %copy.62), calls=%async_computation.1 | async-start | bytes 5111808 | tf_op jit(solution)/shard_map/all_to_all | solution.py:90
  88.1 56.0 %all-to-all-done.1 = f32[16,22,13,128]{3,1,2,0:T(8,128)S(1)} async-done(((f32[16,22,13,128]{3,1,2,0:T(8,128)}), f32[16,22,13,128]{3,1,2,0:T(8,128)S(1)}, u32[]{:S(2)}, u32[]{:S(2)}) %all-to-all-start.1) | async-done | bytes 2342944 | tf_op jit(solution)/shard_map/all_to_all | solution.py:90
  144.6 2.4 %copy.79 = f32[44,8,13,128]{3,1,2,0:T(8,128)} copy(f32[44,8,13,128]{3,2,1,0:T(8,128)S(1)} %bitcast.56) | data formatting | bytes 4685824
  147.1 2.4 %copy.64 = f32[1664,352]{1,0:T(8,128)S(1)} copy(f32[1664,352]{0,1:T(8,128)} %bitcast.58) | data formatting | bytes 4685824 | tf_op jit(solution)/shard_map/st,sk->tk/dot_general | solution.py:104
  149.5 1.3 fusion.26
  (55 shorter events, 11.1 us)
Async XLA Ops:
  0.6 49.9 %copy-start = (f32[12,12]{1,0:T(8,128)S(1)}, f32[12,12]{1,0:T(8,128)}, u32[]{:S(2)}) copy-start(f32[12,12]{1,0:T(8,128)} %param.12) | copy-start | bytes 1732
  0.6 14.0 %copy-start.4 = (s32[8,3600]{1,0:T(8,128)S(1)}, s32[8,3600]{1,0:T(8,128)}, u32[]{:S(2)}) copy-start(s32[8,3600]{1,0:T(8,128)} %param.11) | copy-start | bytes 345604
  0.7 14.0 %copy-start.6 = (f32[8,3600]{1,0:T(8,128)S(1)}, f32[8,3600]{1,0:T(8,128)}, u32[]{:S(2)}) copy-start(f32[8,3600]{1,0:T(8,128)} %param.9) | copy-start | bytes 345604
  6.4 75.6 %all-to-all-start = ((f32[16,1,22]{2,1,0:T(1,128)}), f32[16,1,22]{2,1,0:T(1,128)S(1)}, u32[]{:S(2)}, u32[]{:S(2)}) async-start(f32[16,1,22]{2,1,0:T(1,128)} %all_to_all.9), calls=%async_computation | async-start | bytes 16384 | tf_op jit(solution)/shard_map/all_to_all | solution.py:97
  15.7 10.7 %collective-permute-start.1 = (f32[3,6,1,3600]{3,1,2,0:T(8,128)}, f32[3,6,1,3600]{3,1,2,0:T(8,128)S(1)}, u32[]{:S(2)}, u32[]{:S(2)}) collective-permute-start(f32[3,6,1,3600]{3,1,2,0:T(8,128)} %get-tuple-element.8), channel_id=1, source_target_pairs={{1,0},{2,1},{3,2},{4,3},{5,4},{6,5},{7,6},{8,7},{9,8},{10,9},{11,1... | collective-permute-start | bytes 777608 | tf_op jit(solution)/shard_map/ppermute | solution.py:21
  18.0 8.9 %collective-permute-start = (f32[3,6,1,3600]{3,1,2,0:T(8,128)}, f32[3,6,1,3600]{3,1,2,0:T(8,128)}, u32[]{:S(2)}, u32[]{:S(2)}) collective-permute-start(f32[3,6,1,3600]{3,1,2,0:T(8,128)} %get-tuple-element.9), channel_id=1, source_target_pairs={{0,1},{1,2},{2,3},{3,4},{4,5},{5,6},{6,7},{7,8},{8,9},{9,10},{10,1... | collective-permute-start | bytes 777608 | tf_op jit(solution)/shard_map/ppermute | solution.py:20
  28.5 0.7 copy-start.7
  29.3 1.4 copy-start.1
  29.4 1.9 %copy-start.2 = (f32[2,6,8,3599]{3,1,2,0:T(8,128)S(1)}, f32[2,6,8,3599]{3,1,2,0:T(8,128)}, u32[]{:S(2)}) copy-start(f32[2,6,8,3599]{3,1,2,0:T(8,128)} %slice.177) | copy-start | bytes 4146052
  34.9 8.4 %collective-permute-start.3 = (f32[2,6,1,3600]{3,1,2,0:T(8,128)S(1)}, f32[2,6,1,3600]{3,1,2,0:T(8,128)S(1)}, u32[]{:S(2)}, u32[]{:S(2)}) collective-permute-start(f32[2,6,1,3600]{3,1,2,0:T(8,128)S(1)} %get-tuple-element.10), channel_id=1, source_target_pairs={{0,1},{1,2},{2,3},{3,4},{4,5},{5,6},{6,7},{7,8},{8,9},{9,10},{10,1... | collective-permute-start | bytes 518408 | tf_op jit(solution)/shard_map/ppermute | solution.py:20
  40.3 8.3 %collective-permute-start.2 = (f32[2,6,1,3600]{3,1,2,0:T(8,128)S(1)}, f32[2,6,1,3600]{3,1,2,0:T(8,128)S(1)}, u32[]{:S(2)}, u32[]{:S(2)}) collective-permute-start(f32[2,6,1,3600]{3,1,2,0:T(8,128)S(1)} %get-tuple-element.11), channel_id=1, source_target_pairs={{1,0},{2,1},{3,2},{4,3},{5,4},{6,5},{7,6},{8,7},{9,8},{10,9},{11,1... | collective-permute-start | bytes 518408 | tf_op jit(solution)/shard_map/ppermute | solution.py:21
  50.0 3.7 %copy-start.3 = (f32[2,6,8,3600]{3,2,1,0:T(8,128)}, f32[2,6,8,3600]{3,2,1,0:T(8,128)S(1)}, u32[]{:S(2)}) copy-start(f32[2,6,8,3600]{3,2,1,0:T(8,128)S(1)} %copy.66) | copy-start | bytes 4147204
  50.0 1.0 copy-start.5
  82.0 62.1 %all-to-all-start.1 = ((f32[16,22,13,128]{3,1,2,0:T(8,128)}), f32[16,22,13,128]{3,1,2,0:T(8,128)S(1)}, u32[]{:S(2)}, u32[]{:S(2)}) async-start(f32[16,22,13,128]{3,1,2,0:T(8,128)} %copy.62), calls=%async_computation.1 | async-start | bytes 5111808 | tf_op jit(solution)/shard_map/all_to_all | solution.py:90
where the time goes:
time: 152 us; the launch traced here: 151 us
  waiting for transfers between devices  62.2 us (41%)
  local copies, waits for them, and re-layouts  40.3 us (27%)
  starting transfers between devices  25.3 us (17%)
  other arithmetic  12.3 us (8%)
  matrix products  10.4 us (7%)
    all_to_all x1, waiting for transfers between devices, body(): lax.all_to_all(buffer.reshape(devices, capacity, FIELDS + 1, AT), 'blk',...  56 us
    scatter x1, local copies, waits for them, and re-layouts, body(): jnp.zeros((devices * capacity, FIELDS + 1, AT), jnp.float32).at[position]  17.6 us
    ppermute x2, starting transfers between devices, extended_2(): before = lax.ppermute(last, axis, up)  9.54 us
    unnamed x21, local copies, waits for them, and re-layouts  7.5 us
    all_to_all x1, starting transfers between devices, body(): lax.all_to_all(labels.reshape(devices, capacity), 'blk', split_axis=0, co...  6.55 us
    dot_general x1, matrix products, body(): jnp.einsum('brc,bca->bra', blocks, remap_weights, preferred_element_type=...  6.42 us
    ppermute x2, waiting for transfers between devices, extended_2(): after = lax.ppermute(first, axis, down)  5.3 us
    all_to_all x1, starting transfers between devices, body(): lax.all_to_all(buffer.reshape(devices, capacity, FIELDS + 1, AT), 'blk',...  4.87 us
  transfers between devices with their start and end apart: 6, of which 4 were waited for; matrix products, arithmetic and copies ran while one was open for 31% of the time, Pallas kernels for 0%

commit v1 on v0

v1 whole, which is shorter than its diff:
```python
import functools

import jax
import jax.numpy as jnp
from jax import lax
from jax.experimental import pallas as pl
from jax.experimental.pallas import tpu as pltpu
from jax.sharding import PartitionSpec as P

NZ = 6
FIELDS = 12
CB = 128
AT = 128
NTILE = 8
ROWS = 8
LANES = 128
WIDE = 16
HIGH = lax.Precision.HIGHEST


def lane_pair(cur, before, after, lane):
    east = pltpu.roll(jnp.where(lane == 0, after, cur), LANES - 1, 1)
    west = pltpu.roll(jnp.where(lane == LANES - 1, before, cur), 1, 1)
    return east, west


def row_pair(cur, other, sub):
    up = pltpu.roll(jnp.where(sub == ROWS - 1, other, cur), 1, 0)
    down = pltpu.roll(jnp.where(sub == 0, other, cur), ROWS - 1, 0)
    return up, down


def faces(kap, wet, other_kap, other_wet, lane, sub):
    cur, wcur = kap[0], wet[0]
    nbk = lane_pair(*kap, lane) + row_pair(cur, other_kap, sub)
    nbw = lane_pair(*wet, lane) + row_pair(wcur, other_wet, sub)
    return [(jnp.sqrt(cur * k), jnp.minimum(wcur, w)) for k, w in zip(nbk, nbw)]


def mixed(tiles, others, face, wet, kv, lane, sub):
    out = [[None] * NZ for _ in range(2)]
    for l in range(NZ):
        coef = [jnp.where(l < depth, root, 0.0) for root, depth in face]
        below = jnp.where(l + 1 < wet, kv[l], 0.0) if l + 1 < NZ else None
        above = jnp.where(l < wet, kv[l - 1], 0.0) if l > 0 else None
        for c in range(2):
            cur = tiles[c][l][0]
            near = lane_pair(*tiles[c][l], lane) + row_pair(cur, others[c][l], sub)
            change = coef[0] * (near[0] - cur)
            for a, v in zip(coef[1:], near[1:]):
                change = change + a * (v - cur)
            if below is not None:
                change = change + below * (tiles[c][l + 1][0] - cur)
            if above is not None:
                change = change + above * (tiles[c][l - 1][0] - cur)
            out[c][l] = cur + change
    return out


def local_kernel(
    u_ref, kap_ref, wet_ref, halo_ref, kv_ref, coup_ref, dest_ref, tile_ref, w_hbm,
    next_ref, sums_ref,
    full, mid, surf, blocks, acc, weights, w_sem,
):
    length = u_ref.shape[-1]
    count = w_hbm.shape[0]
    tiles = full.shape[-1] // LANES
    last = tiles - 1
    rem = length - last * LANES
    cut = last * LANES
    fetch = pltpu.make_async_copy(w_hbm, weights, w_sem)
    fetch.start()

    lane = lax.broadcasted_iota(jnp.int32, (ROWS, LANES), 1)
    sub = lax.broadcasted_iota(jnp.int32, (ROWS, LANES), 0)
    kv = [kv_ref[l] for l in range(NZ)]

    def place(side, q, value):
        full[side, q, :, 0:cut] = value[:, 0:cut]
        tail = jnp.concatenate(
            [value[:, cut:length], jnp.zeros((ROWS, LANES - rem), jnp.float32)], axis=1
        )
        half = rem + (LANES - rem) // 2
        tail = jnp.where(
            lane < rem,
            tail,
            jnp.where(
                lane < half,
                pltpu.roll(value[:, 0:LANES], rem, 1),
                pltpu.roll(tail, LANES - rem, 1),
            ),
        )
        full[side, q, :, cut:] = tail

    for c in range(2):
        for l in range(NZ):
            place(0, c * NZ + l, u_ref[c, l])
    place(0, 12, kap_ref[...])
    place(0, 13, wet_ref[...].astype(jnp.float32))
    for q in range(14):
        place(1, q, halo_ref[q])
    acc[...] = jnp.zeros_like(acc)

    def columns(t):
        def at(i):
            return pl.ds(pl.multiple_of(i * LANES, LANES), LANES)

        return [at(t), at(lax.rem(t + last, tiles)), at(lax.rem(t + 1, tiles))]

    def first(t, carry):
        cols = columns(t)
        get = lambda side, q: [full[side, q, :, s] for s in cols]
        state = [[[get(side, c * NZ + l) for l in range(NZ)] for c in range(2)] for side in range(2)]
        kap = [get(side, 12) for side in range(2)]
        wet = [get(side, 13) for side in range(2)]
        for side in range(2):
            o = 1 - side
            face = faces(kap[side], wet[side], kap[o][0], wet[o][0], lane, sub)
            others = [[state[o][c][l][0] for l in range(NZ)] for c in range(2)]
            new = mixed(state[side], others, face, wet[side][0], kv, lane, sub)
            for c in range(2):
                for l in range(NZ):
                    mid[side, c * NZ + l, :, cols[0]] = new[c][l]
        return carry

    lax.fori_loop(0, tiles, first, 0)

    big = ROWS * WIDE
    inner = (FIELDS + 1) * ROWS
    r0 = lax.broadcasted_iota(jnp.int32, (big, FIELDS), 0)
    r1 = lax.broadcasted_iota(jnp.int32, (big, FIELDS), 1)
    pick_f = jnp.where(lax.rem(r0, WIDE) == r1, 1.0, 0.0)
    q0 = lax.broadcasted_iota(jnp.int32, (FIELDS, inner), 0)
    q1 = lax.broadcasted_iota(jnp.int32, (FIELDS, inner), 1)
    pick_q = jnp.where(q1 // ROWS == q0, 1.0, 0.0)
    spread = jnp.dot(
        jnp.dot(pick_f, coup_ref[...], precision=HIGH, preferred_element_type=jnp.float32),
        pick_q, precision=HIGH, preferred_element_type=jnp.float32,
    )
    m0 = lax.broadcasted_iota(jnp.int32, (big, inner), 0)
    m1 = lax.broadcasted_iota(jnp.int32, (big, inner), 1)
    same = (m0 // WIDE) == lax.rem(m1, ROWS)
    sea_entry = (lax.rem(m0, WIDE) == FIELDS) & (m1 // ROWS == FIELDS)
    spread = jnp.where(same, jnp.where(sea_entry, 1.0, spread), 0.0)

    def second(t):
        cols = columns(t)
        get = lambda ref, side, q: [ref[side, q, :, s] for s in cols]
        state = [[get(mid, 0, c * NZ + l) for l in range(NZ)] for c in range(2)]
        others = [[mid[1, c * NZ + l, :, cols[0]] for l in range(NZ)] for c in range(2)]
        kap, wet = get(full, 0, 12), get(full, 0, 13)
        face = faces(kap, wet, full[1, 12, :, cols[0]], full[1, 13, :, cols[0]], lane, sub)
        new = mixed(state, others, face, wet[0], kv, lane, sub)
        sea = jnp.where(wet[0] > 0.0, 1.0, 0.0)
        rows = [new[c][l] * sea for c in range(2) for l in range(NZ)] + [sea]
        surf[:, cols[0]] = jnp.dot(
            spread, jnp.concatenate(rows, axis=0), precision=HIGH,
            preferred_element_type=jnp.float32,
        )
        return new, cols[0]

    def second_loop(t, carry):
        new, here = second(t)
        for c in range(2):
            for l in range(NZ):
                next_ref[c, l, :, here] = new[c][l]
        return carry

    lax.fori_loop(0, last, second_loop, 0)
    new, _ = second(last)
    for c in range(2):
        for l in range(NZ):
            next_ref[c, l, :, cut:length] = new[c][l][:, 0:rem]

    wlane = lax.broadcasted_iota(jnp.int32, (WIDE, LANES), 1)

    def shifted(j, cur, before):
        shift = rem * j
        if shift == 0:
            return cur
        return pltpu.roll(jnp.where(wlane < LANES - shift, cur, before), shift, 1)

    def align(t, carry):
        here = pl.ds(pl.multiple_of(t * LANES, LANES), LANES)
        prev = pl.ds(pl.multiple_of((t - 1) * LANES, LANES), LANES)
        for j in range(ROWS):
            rows = pl.ds(j * WIDE, WIDE)
            value = shifted(j, surf[rows, here], surf[rows, prev])
            blocks[last * j + t] = value.astype(jnp.bfloat16)
        return carry

    lax.fori_loop(1, last, align, 0)
    for j in range(ROWS + 1):
        if j > 0:
            rows = pl.ds((j - 1) * WIDE, WIDE)
            tail = shifted(j - 1, surf[rows, cut:cut + LANES], surf[rows, cut - LANES:cut])
        if j < ROWS:
            head = surf[pl.ds(j * WIDE, WIDE), 0:LANES]
            if j > 0:
                head = jnp.where(wlane >= rem * j, pltpu.roll(head, rem * j, 1), tail)
        else:
            head = tail
        blocks[last * j] = head.astype(jnp.bfloat16)

    fetch.wait()

    def product(g, carry):
        value = jnp.dot(blocks[g], weights[g], preferred_element_type=jnp.float32)
        seg = dest_ref[g] * NTILE + tile_ref[g]
        here = pl.ds(pl.multiple_of(seg * WIDE, WIDE), WIDE)
        acc[here, :] = acc[here, :] + value
        return carry

    lax.fori_loop(0, count, product, 0, unroll=9)

    owners = sums_ref.shape[0]
    quarter = owners // 4

    def deliver(d, carry):
        slot = lax.rem(d, 4)
        slot = (lax.rem(slot, 2) * 2 + slot // 2) * quarter + d // 4
        for r in range(FIELDS + 1):
            sums_ref[slot, r] = acc[pl.ds(d * (NTILE * WIDE) + r, NTILE, stride=WIDE), :]
        return carry

    lax.fori_loop(0, owners, deliver, 0)


def local_part(u, kap, wet, halo, kv, coup, dest, tile, weights, owners):
    length = u.shape[-1]
    pad = -(-length // LANES) * LANES
    count = weights.shape[0]
    vmem = pl.BlockSpec(memory_space=pltpu.VMEM)
    smem = pl.BlockSpec(memory_space=pltpu.SMEM)
    return pl.pallas_call(
        local_kernel,
        name="mix_and_remap",
        out_shape=(
            jax.ShapeDtypeStruct(u.shape, jnp.float32),
            jax.ShapeDtypeStruct((owners, FIELDS + 1, NTILE, AT), jnp.float32),
        ),
        in_specs=[vmem, vmem, vmem, vmem, smem, vmem, smem, smem, pl.BlockSpec(memory_space=pl.ANY)],
        out_specs=(vmem, vmem),
        scratch_shapes=[
            pltpu.VMEM((2, 14, ROWS, pad), jnp.float32),
            pltpu.VMEM((2, 12, ROWS, pad), jnp.float32),
            pltpu.VMEM((ROWS * WIDE, pad), jnp.float32),
            pltpu.VMEM((count, WIDE, CB), jnp.bfloat16),
            pltpu.VMEM((owners * NTILE * WIDE, AT), jnp.float32),
            pltpu.VMEM(weights.shape, jnp.bfloat16),
            pltpu.SemaphoreType.DMA,
        ],
        compiler_params=pltpu.CompilerParams(vmem_limit_bytes=44 * 2**20),
    )(u, kap, wet, halo, kv, coup, dest, tile, weights)


PARTS = ((0, 7), (7, 13))


def owner_kernel(n, sums_ref, out_ref, sum1, sum2, got1, got2, got3, ratio, send, recv):
    me = lax.axis_index("blk")
    quarter = n // 4
    core, side, q = lax.rem(me, 2), lax.rem(me // 2, 2), me // 4
    mate1 = me + 1 - 2 * core
    mate2 = me + 2 - 4 * side
    line = [(lax.rem(q + k, quarter)) * 4 + lax.rem(me, 4) for k in range(1, quarter)]

    barrier = pltpu.get_barrier_semaphore()
    for other in [mate1, mate2] + line:
        pl.semaphore_signal(
            barrier, inc=1, device_id={"blk": other}, device_id_type=pl.DeviceIdType.MESH
        )
    pl.semaphore_wait(barrier, 1 + quarter)

    def copy(src, dst, index, other):
        return pltpu.make_async_remote_copy(
            src_ref=src, dst_ref=dst, send_sem=send.at[index], recv_sem=recv.at[index],
            device_id={"blk": other}, device_id_type=pl.DeviceIdType.MESH,
        )

    np_ = len(PARTS)
    ones, twos, threes = [], [], []
    for i, (a, b) in enumerate(PARTS):
        rows = pl.ds(a, b - a)
        ones.append(copy(sums_ref.at[1 - core, :, :, rows], got1.at[:, :, rows], i, mate1))
        ones[-1].start()
    for i, (a, b) in enumerate(PARTS):
        rows = pl.ds(a, b - a)
        ones[i].wait_recv()
        sum1[:, :, rows] = sums_ref[core, :, :, rows] + got1[:, :, rows]
        twos.append(copy(sum1.at[1 - side, :, rows], got2.at[:, rows], np_ + i, mate2))
        twos[-1].start()
    for i, (a, b) in enumerate(PARTS):
        rows = pl.ds(a, b - a)
        twos[i].wait_recv()
        sum2[:, rows] = sum1[side, :, rows] + got2[:, rows]
        threes.append([])
        for k in range(1, quarter):
            to = lax.rem(q + k, quarter)
            threes[i].append(
                copy(sum2.at[to, rows], got3.at[k - 1, rows], 2 * np_ + (k - 1) * np_ + i, line[k - 1])
            )
            threes[i][-1].start()
    total = []
    for i, (a, b) in enumerate(PARTS):
        rows = pl.ds(a, b - a)
        value = sum2[q, rows]
        for k in range(1, quarter):
            threes[i][k - 1].wait_recv()
            value = value + got3[k - 1, rows]
        total.append(value)
    total = jnp.concatenate(total, axis=0)
    below = jnp.maximum(total[FIELDS], 1.0)
    for f in range(FIELDS):
        ratio[f * NTILE:(f + 1) * NTILE, :] = total[f] / below
    for t in range(NTILE):
        out_ref[:, t * AT:(t + 1) * AT] = ratio[pl.ds(t, FIELDS, stride=NTILE), :]
    for group in [ones, twos] + threes:
        for one in group:
            one.wait_send()


def owner_part(sums):
    n = sums.shape[0]
    quarter = n // 4
    block = sums.shape[1:]
    slots = (2 + quarter) * len(PARTS)
    vmem = pl.BlockSpec(memory_space=pltpu.VMEM)
    return pl.pallas_call(
        functools.partial(owner_kernel, n),
        name="owner_sums",
        out_shape=jax.ShapeDtypeStruct((FIELDS, NTILE * AT), jnp.float32),
        in_specs=[vmem],
        out_specs=vmem,
        scratch_shapes=[
            pltpu.VMEM((2, quarter) + block, jnp.float32),
            pltpu.VMEM((quarter,) + block, jnp.float32),
            pltpu.VMEM((2, quarter) + block, jnp.float32),
            pltpu.VMEM((quarter,) + block, jnp.float32),
            pltpu.VMEM((max(1, quarter - 1),) + block, jnp.float32),
            pltpu.VMEM((FIELDS * NTILE, AT), jnp.float32),
            pltpu.SemaphoreType.DMA((slots,)),
            pltpu.SemaphoreType.DMA((slots,)),
        ],
        compiler_params=pltpu.CompilerParams(
            collective_id=0, has_side_effects=True, vmem_limit_bytes=40 * 2**20
        ),
    )(sums.reshape((2, 2, quarter) + block))


def body(
    ocean_state, kappa_h, kappa_v, wet_depth, coupling, dest_of_block, tile_of_block, remap_weights
):
    size = lax.axis_size("blk")
    length = ocean_state.shape[-1]
    stacked = jnp.concatenate(
        [
            ocean_state.reshape(2 * NZ, ROWS, length),
            kappa_h[None],
            wet_depth.astype(jnp.float32)[None],
        ],
        axis=0,
    )
    up = [(i, i + 1) for i in range(size - 1)]
    down = [(i + 1, i) for i in range(size - 1)]
    before = lax.ppermute(stacked[:, ROWS - 2:], "blk", up)
    after = lax.ppermute(stacked[:, :2], "blk", down)
    zeros = jnp.zeros((2 * NZ + 2, ROWS - 4, length), jnp.float32)
    halo = jnp.concatenate([after, zeros, before], axis=1)
    ocean_next, sums = local_part(
        ocean_state, kappa_h, wet_depth, halo, kappa_v, coupling,
        dest_of_block.reshape(-1), tile_of_block, remap_weights, size,
    )
    return ocean_next, owner_part(sums)


def solution(mesh):
    return jax.shard_map(
        body,
        mesh=mesh,
        in_specs=(
            P(None, None, ("groups", "blk"), None),
            P("blk", None),
            P(),
            P("blk", None),
            P(),
            P("blk", None),
            P("blk"),
            P("blk", None, None),
        ),
        out_specs=(P(None, None, ("groups", "blk"), None), P(None, ("groups", "blk"))),
        check_vma=False,
    )
```

time: 152 us -> 59.3 us (0.39)
  the two profiles are of different devices: /device:TPU:13 before, /device:TPU:0 now
where the time goes in v1:
time: 59.3 us; the launch traced here: 59.1 us
  Pallas kernels  48.3 us (81%)
  starting transfers between devices  4.48 us (8%)
  other arithmetic  3.51 us (6%)
  waiting for transfers between devices  1.25 us (2%)
  between operations  0.79 us (1%)
  local copies, waits for them, and re-layouts  0.75 us (1%)
    pallas_call x1, Pallas kernels, owner_part(): pl.pallas_call(functools.partial(owner_kernel, n), name='owner_sums', out...  25.2 us
    pallas_call x1, Pallas kernels, local_part(): pl.pallas_call(local_kernel, name='mix_and_remap', out_shape=(jax.ShapeDt...  23.1 us
    ppermute x1, starting transfers between devices, body(): before = lax.ppermute(stacked[:, ROWS - 2:], 'blk', up)  3.06 us
    slice x1, other arithmetic, body(): after = lax.ppermute(stacked[:, :2], 'blk', down)  2.21 us
    ppermute x1, starting transfers between devices, body(): after = lax.ppermute(stacked[:, :2], 'blk', down)  1.42 us
    ppermute x1, waiting for transfers between devices, body(): before = lax.ppermute(stacked[:, ROWS - 2:], 'blk', up)  1.25 us
  transfers between devices with their start and end apart: 2, of which 1 were waited for; matrix products, arithmetic and copies ran while one was open for 0% of the time, Pallas kernels for 0%

profile of v1, /device:TPU:0, one launch (start us, length us, event | category | flops | bytes accessed | tf_op | source)
XLA Modules:
  0.0 59.1 jit_solution(8889100286466394305)
XLA Ops:
  0.6 0.9 %convert_bitcast_fusion = f32[1,8,3600]{2,1,0:T(8,128)S(1)} fusion(s32[8,3600]{1,0:T(8,128)} %wet_ref.1), kind=kLoop, calls=%fused_computation.4 | loop fusion | flops 28800 | bytes 230400 | tf_op jit(solution)/shard_map/broadcast_in_dim | solution.py:360
  1.5 2.2 %pad_maximum_fusion.3 = (f32[14,2,3600]{2,1,0:T(2,128)S(1)}, f32[14,2,3600]{2,1,0:T(2,128)S(1)}) fusion(f32[1,8,3600]{2,1,0:T(8,128)S(1)} %convert_bitcast_fusion, f32[1,8,3600]{2,1,0:T(8,128)} %bitcast.8, f32[12,8,3600]{2,1,0:T(8,128)} %bitcast.6), kind=kLoop, calls=%fused_computation.3 | loop fusion | flops 403200 | bytes 2419200 | tf_op jit(solution)/shard_map/slice | solution.py:367
  3.8 0.0 copy-start
  3.8 0.0 copy-start.1
  3.8 0.0 copy-start.2
  3.8 0.0 copy-start.3
  3.8 0.0 copy-start.4
  3.8 0.0 copy-start.5
  3.8 0.0 copy-start.6
  3.8 1.4 %collective-permute-start = (f32[14,2,3600]{2,1,0:T(2,128)S(1)}, f32[14,2,3600]{2,1,0:T(2,128)S(1)}, u32[]{:S(2)}, u32[]{:S(2)}) collective-permute-start(f32[14,2,3600]{2,1,0:T(2,128)S(1)} %get-tuple-element.6), channel_id=1, source_target_pairs={{1,0},{2,1},{3,2},{4,3},{5,4},{6,5},{7,6},{8,7},{9,8},{10,9},{11,1... | collective-permute-start | bytes 1209608 | tf_op jit(solution)/shard_map/ppermute | solution.py:367
  5.3 3.1 %collective-permute-start.1 = (f32[14,2,3600]{2,1,0:T(2,128)S(1)}, f32[14,2,3600]{2,1,0:T(2,128)S(1)}, u32[]{:S(2)}, u32[]{:S(2)}) collective-permute-start(f32[14,2,3600]{2,1,0:T(2,128)S(1)} %get-tuple-element.7), channel_id=1, source_target_pairs={{0,1},{1,2},{2,3},{3,4},{4,5},{5,6},{6,7},{7,8},{8,9},{9,10},{10,1... | collective-permute-start | bytes 1209608 | tf_op jit(solution)/shard_map/ppermute | solution.py:366
  8.4 0.1 pad.1.clone
  8.4 0.0 collective-permute-done
  8.4 1.2 %collective-permute-done.1 = f32[14,2,3600]{2,1,0:T(2,128)S(1)} collective-permute-done((f32[14,2,3600]{2,1,0:T(2,128)S(1)}, f32[14,2,3600]{2,1,0:T(2,128)S(1)}, u32[]{:S(2)}, u32[]{:S(2)}) %collective-permute-start.1) | collective-permute-done | bytes 403232 | tf_op jit(solution)/shard_map/ppermute | solution.py:366
  9.7 0.4 pad_maximum_fusion.halo_ref
  10.1 0.0 copy-done
  10.1 0.0 copy-done.1
  10.1 0.0 copy-done.2
  10.1 0.0 copy-done.3
  10.1 0.0 copy-done.4
  10.1 0.0 copy-done.5
  10.1 0.0 copy-done.6
  10.1 23.1 %mix_and_remap.1 = (f32[2,6,8,3600]{3,2,1,0:T(8,128)}, f32[16,13,8,128]{3,2,1,0:T(8,128)S(1)}) custom-call(f32[2,6,8,3600]{3,2,1,0:T(8,128)S(1)} %copy-done, f32[8,3600]{1,0:T(8,128)S(1)} %copy-done.2, s32[8,3600]{1,0:T(8,128)S(1)} %copy-done.1, f32[14,8,3600]{2,1,0:T(8,128)S(1)} %pad_maximum_fusion.halo_ref, f32[6]{0:T(128)S(1)} %copy-done.6, ...), custom_call_target="tpu_custom_call" | custom-call | tf_op jit(solution)/shard_map/mix_and_remap/pallas_call | solution.py:235
  33.3 25.2 %owner_sums.1 = f32[12,1024]{1,0:T(8,128)S(1)} custom-call(f32[2,2,4,13,8,128]{5,4,3,2,1,0:T(8,128)S(1)} %bitcast.7), custom_call_target="tpu_custom_call" | custom-call | tf_op jit(solution)/shard_map/owner_sums/pallas_call | solution.py:329
  58.5 0.6 %copy.11 = f32[12,1024]{1,0:T(8,128)} copy(f32[12,1024]{1,0:T(8,128)S(1)} %owner_sums.1) | data formatting | bytes 98304
  (1 shorter events, 0.0 us)
Async XLA Ops:
  3.8 6.3 %copy-start = (f32[2,6,8,3600]{3,2,1,0:T(8,128)S(1)}, f32[2,6,8,3600]{3,2,1,0:T(8,128)}, u32[]{:S(2)}) copy-start(f32[2,6,8,3600]{3,2,1,0:T(8,128)} %u_ref.1) | copy-start | bytes 4147204
  3.8 6.3 %copy-start.1 = (s32[8,3600]{1,0:T(8,128)S(1)}, s32[8,3600]{1,0:T(8,128)}, u32[]{:S(2)}) copy-start(s32[8,3600]{1,0:T(8,128)} %wet_ref.1) | copy-start | bytes 345604
  3.8 6.3 %copy-start.2 = (f32[8,3600]{1,0:T(8,128)S(1)}, f32[8,3600]{1,0:T(8,128)}, u32[]{:S(2)}) copy-start(f32[8,3600]{1,0:T(8,128)} %kap_ref.1) | copy-start | bytes 345604
  3.8 6.3 %copy-start.3 = (f32[12,12]{1,0:T(8,128)S(1)}, f32[12,12]{1,0:T(8,128)}, u32[]{:S(2)}) copy-start(f32[12,12]{1,0:T(8,128)} %coup_ref.1) | copy-start | bytes 1732
  3.8 6.3 %copy-start.4 = (s32[225,1]{0,1:T(1,128)S(1)}, s32[225,1]{0,1:T(1,128)}, u32[]{:S(2)}) copy-start(s32[225,1]{0,1:T(1,128)} %param.13) | copy-start | bytes 2704
  3.8 6.3 %copy-start.5 = (s32[225]{0:T(256)S(1)}, s32[225]{0:T(256)}, u32[]{:S(2)}) copy-start(s32[225]{0:T(256)} %tile_ref.1) | copy-start | bytes 2704
  3.8 6.3 %copy-start.6 = (f32[6]{0:T(128)S(1)}, f32[6]{0:T(128)}, u32[]{:S(2)}) copy-start(f32[6]{0:T(128)} %kv_ref.1) | copy-start | bytes 76
  3.8 4.6 %collective-permute-start = (f32[14,2,3600]{2,1,0:T(2,128)S(1)}, f32[14,2,3600]{2,1,0:T(2,128)S(1)}, u32[]{:S(2)}, u32[]{:S(2)}) collective-permute-start(f32[14,2,3600]{2,1,0:T(2,128)S(1)} %get-tuple-element.6), channel_id=1, source_target_pairs={{1,0},{2,1},{3,2},{4,3},{5,4},{6,5},{7,6},{8,7},{9,8},{10,9},{11,1... | collective-permute-start | bytes 1209608 | tf_op jit(solution)/shard_map/ppermute | solution.py:367
  5.3 4.4 %collective-permute-start.1 = (f32[14,2,3600]{2,1,0:T(2,128)S(1)}, f32[14,2,3600]{2,1,0:T(2,128)S(1)}, u32[]{:S(2)}, u32[]{:S(2)}) collective-permute-start(f32[14,2,3600]{2,1,0:T(2,128)S(1)} %get-tuple-element.7), channel_id=1, source_target_pairs={{0,1},{1,2},{2,3},{3,4},{4,5},{5,6},{6,7},{7,8},{8,9},{9,10},{10,1... | collective-permute-start | bytes 1209608 | tf_op jit(solution)/shard_map/ppermute | solution.py:366

commit v2 on v1

--- a/solution.py
+++ b/solution.py
@@ -35,6 +35,11 @@
     nbk = lane_pair(*kap, lane) + row_pair(cur, other_kap, sub)
     nbw = lane_pair(*wet, lane) + row_pair(wcur, other_wet, sub)
     return [(jnp.sqrt(cur * k), jnp.minimum(wcur, w)) for k, w in zip(nbk, nbw)]
+
+
+def halves(x):
+    hi = x.astype(jnp.bfloat16)
+    return hi, (x - hi.astype(jnp.float32)).astype(jnp.bfloat16)
 
 
 def mixed(tiles, others, face, wet, kv, lane, sub):
@@ -58,7 +63,7 @@
 
 
 def local_kernel(
-    u_ref, kap_ref, wet_ref, halo_ref, kv_ref, coup_ref, dest_ref, tile_ref, w_hbm,
+    u_ref, kap_ref, wet_ref, halo_u, halo_kap, halo_wet, kv_ref, coup_ref, dest_ref, tile_ref, w_hbm,
     next_ref, sums_ref,
     full, mid, surf, blocks, acc, weights, w_sem,
 ):
@@ -97,8 +102,11 @@
             place(0, c * NZ + l, u_ref[c, l])
     place(0, 12, kap_ref[...])
     place(0, 13, wet_ref[...].astype(jnp.float32))
-    for q in range(14):
-        place(1, q, halo_ref[q])
+    for c in range(2):
+        for l in range(NZ):
+            place(1, c * NZ + l, halo_u[c, l])
+    place(1, 12, halo_kap[...])
+    place(1, 13, halo_wet[...].astype(jnp.float32))
     acc[...] = jnp.zeros_like(acc)
 
     def columns(t):
@@ -142,6 +150,8 @@
     same = (m0 // WIDE) == lax.rem(m1, ROWS)
     sea_entry = (lax.rem(m0, WIDE) == FIELDS) & (m1 // ROWS == FIELDS)
     spread = jnp.where(same, jnp.where(sea_entry, 1.0, spread), 0.0)
+    spread_hi, spread_lo = halves(spread)
+    spread3 = jnp.concatenate([spread_hi, spread_hi, spread_lo], axis=1)
 
     def second(t):
         cols = columns(t)
@@ -153,21 +163,29 @@
         new = mixed(state, others, face, wet[0], kv, lane, sub)
         sea = jnp.where(wet[0] > 0.0, 1.0, 0.0)
         rows = [new[c][l] * sea for c in range(2) for l in range(NZ)] + [sea]
-        surf[:, cols[0]] = jnp.dot(
-            spread, jnp.concatenate(rows, axis=0), precision=HIGH,
-            preferred_element_type=jnp.float32,
-        )
-        return new, cols[0]
-
-    def second_loop(t, carry):
-        new, here = second(t)
-        for c in range(2):
-            for l in range(NZ):
-                next_ref[c, l, :, here] = new[c][l]
+        return new, cols[0], jnp.concatenate(rows, axis=0)
+
+    def couple(profile):
+        hi, lo = halves(profile)
+        return jnp.dot(
+            spread3, jnp.concatenate([hi, lo, hi], axis=0), preferred_element_type=jnp.float32
+        )
+
+    def second_loop(p, carry):
+        profiles = []
+        for k in range(2):
+            new, here, profile = second(2 * p + k)
+            profiles.append(profile)
+            for c in range(2):
+                for l in range(NZ):
+                    next_ref[c, l, :, here] = new[c][l]
+        here = pl.ds(pl.multiple_of(p * (2 * LANES), LANES), 2 * LANES)
+        surf[:, here] = couple(jnp.concatenate(profiles, axis=1))
         return carry
 
-    lax.fori_loop(0, last, second_loop, 0)
-    new, _ = second(last)
+    lax.fori_loop(0, last // 2, second_loop, 0)
+    new, here, profile = second(last)
+    surf[:, here] = couple(profile)
     for c in range(2):
         for l in range(NZ):
             next_ref[c, l, :, cut:length] = new[c][l][:, 0:rem]
@@ -189,7 +207,7 @@
             blocks[last * j + t] = value.astype(jnp.bfloat16)
         return carry
 
-    lax.fori_loop(1, last, align, 0)
+    lax.fori_loop(1, last, align, 0, unroll=3)
     for j in range(ROWS + 1):
         if j > 0:
             rows = pl.ds((j - 1) * WIDE, WIDE)
@@ -211,7 +229,7 @@
         acc[here, :] = acc[here, :] + value
         return carry
 
-    lax.fori_loop(0, count, product, 0, unroll=9)
+    lax.fori_loop(0, count, product, 0, unroll=25)
 
     owners = sums_ref.shape[0]
     quarter = owners // 4
@@ -226,7 +244,65 @@
     lax.fori_loop(0, owners, deliver, 0)
 
 
-def local_part(u, kap, wet, halo, kv, coup, dest, tile, weights, owners):
+def halo_kernel(n, *refs):
+    sources, targets, (send, recv) = refs[:3], refs[3:6], refs[6:]
+    me = lax.axis_index("blk")
+    for target in targets:
+        target[...] = jnp.zeros_like(target)
+
+    barrier = pltpu.get_barrier_semaphore()
+    sides = [(me > 0, me - 1, 0), (me < n - 1, me + 1, ROWS - 2)]
+    for other in (lax.rem(me + n - 1, n), lax.rem(me + 1, n)):
+        pl.semaphore_signal(
+            barrier, inc=1, device_id={"blk": other}, device_id_type=pl.DeviceIdType.MESH
+        )
+    pl.semaphore_wait(barrier, 2)
+
+    def copies(i):
+        _, other, row = sides[i]
+        found = []
+        for k, (source, target) in enumerate(zip(sources, targets)):
+            lead = (slice(None),) * (len(source.shape) - 2) + (pl.ds(row, 2),)
+            found.append(pltpu.make_async_remote_copy(
+                src_ref=source.at[lead], dst_ref=target.at[lead],
+                send_sem=send.at[3 * i + k], recv_sem=recv.at[3 * i + k],
+                device_id={"blk": other}, device_id_type=pl.DeviceIdType.MESH,
+            ))
+        return found
+
+    for i in range(2):
+        @pl.when(sides[i][0])
+        def _():
+            for one in copies(i):
+                one.start()
+    for i in range(2):
+        @pl.when(sides[1 - i][0])
+        def _():
+            for one in copies(i):
+                one.wait_recv()
+    for i in range(2):
+        @pl.when(sides[i][0])
+        def _():
+            for one in copies(i):
+                one.wait_send()
+
+
+def halo_part(u, kap, wet, n):
+    vmem = pl.BlockSpec(memory_space=pltpu.VMEM)
+    return pl.pallas_call(
+        functools.partial(halo_kernel, n),
+        name="halo_rows",
+        out_shape=tuple(jax.ShapeDtypeStruct(x.shape, x.dtype) for x in (u, kap, wet)),
+        in_specs=[pl.BlockSpec(memory_space=pl.ANY)] * 3,
+        out_specs=(vmem,) * 3,
+        scratch_shapes=[pltpu.SemaphoreType.DMA((6,)), pltpu.SemaphoreType.DMA((6,))],
+        compiler_params=pltpu.CompilerParams(
+            collective_id=1, has_side_effects=True, vmem_limit_bytes=16 * 2**20
+        ),
+    )(u, kap, wet)
+
+
+def local_part(u, kap, wet, halo_u, halo_kap, halo_wet, kv, coup, dest, tile, weights, owners):
     length = u.shape[-1]
     pad = -(-length // LANES) * LANES
     count = weights.shape[0]
@@ -239,7 +315,7 @@
             jax.ShapeDtypeStruct(u.shape, jnp.float32),
             jax.ShapeDtypeStruct((owners, FIELDS + 1, NTILE, AT), jnp.float32),
         ),
-        in_specs=[vmem, vmem, vmem, vmem, smem, vmem, smem, smem, pl.BlockSpec(memory_space=pl.ANY)],
+        in_specs=[vmem] * 6 + [smem, vmem, smem, smem, pl.BlockSpec(memory_space=pl.ANY)],
         out_specs=(vmem, vmem),
         scratch_shapes=[
             pltpu.VMEM((2, 14, ROWS, pad), jnp.float32),
@@ -251,7 +327,7 @@
             pltpu.SemaphoreType.DMA,
         ],
         compiler_params=pltpu.CompilerParams(vmem_limit_bytes=44 * 2**20),
-    )(u, kap, wet, halo, kv, coup, dest, tile, weights)
+    )(u, kap, wet, halo_u, halo_kap, halo_wet, kv, coup, dest, tile, weights)
 
 
 PARTS = ((0, 7), (7, 13))
@@ -352,23 +428,9 @@
     ocean_state, kappa_h, kappa_v, wet_depth, coupling, dest_of_block, tile_of_block, remap_weights
 ):
     size = lax.axis_size("blk")
-    length = ocean_state.shape[-1]
-    stacked = jnp.concatenate(
-        [
-            ocean_state.reshape(2 * NZ, ROWS, length),
-            kappa_h[None],
-            wet_depth.astype(jnp.float32)[None],
-        ],
-        axis=0,
-    )
-    up = [(i, i + 1) for i in range(size - 1)]
-    down = [(i + 1, i) for i in range(size - 1)]
-    before = lax.ppermute(stacked[:, ROWS - 2:], "blk", up)
-    after = lax.ppermute(stacked[:, :2], "blk", down)
-    zeros = jnp.zeros((2 * NZ + 2, ROWS - 4, length), jnp.float32)
-    halo = jnp.concatenate([after, zeros, before], axis=1)
+    halo = halo_part(ocean_state, kappa_h, wet_depth, size)
     ocean_next, sums = local_part(
-        ocean_state, kappa_h, wet_depth, halo, kappa_v, coupling,
+        ocean_state, kappa_h, wet_depth, *halo, kappa_v, coupling,
         dest_of_block.reshape(-1), tile_of_block, remap_weights, size,
     )
     return ocean_next, owner_part(sums)

time: 59.3 us -> 49.4 us (0.83)
  starting transfers between devices: 4.48 us -> 0 us
  Pallas kernels: 48.3 us -> 44.6 us
  other arithmetic: 3.51 us -> 0 us
  local copies, waits for them, and re-layouts: 0.75 us -> 3.82 us
  waiting for transfers between devices: 1.25 us -> 0 us
    pallas_call x1, Pallas kernels: 23.1 us -> 15.9 us  [local_part(): pl.pallas_call(local_kernel, name='mix_and_remap', out_shape=(jax.ShapeDt...]
    pallas_call x0 -> x1, Pallas kernels: none -> 7.05 us  [halo_part(): pl.pallas_call(functools.partial(halo_kernel, n), name='halo_rows', out_s...]
    ppermute x2 -> x0, starting transfers between devices: 4.48 us -> none  [the longest x1 3.06 us: body(): before = lax.ppermute(stacked[:, ROWS - 2:], 'blk', up)]
    pallas_call x1, Pallas kernels: 25.2 us -> 21.7 us  [owner_part(): pl.pallas_call(functools.partial(owner_kernel, n), name='owner_sums', out...]
    unnamed x15 -> x19, local copies, waits for them, and re-layouts: 0.68 us -> 3.82 us
    slice x1 -> x0, other arithmetic: 2.21 us -> none  [body(): after = lax.ppermute(stacked[:, :2], 'blk', down)]
    ppermute x2 -> x0, waiting for transfers between devices: 1.25 us -> none  [the longest x1 1.25 us: body(): before = lax.ppermute(stacked[:, ROWS - 2:], 'blk', up)]
    broadcast_in_dim x1 -> x0, other arithmetic: 0.91 us -> none  [body(): wet_depth.astype(jnp.float32)[None]]
  transfers between devices with their start and end apart: 2 -> 0, of which waited for: 1 -> 0; matrix products, arithmetic and copies ran while one was open for 0% -> 0% of each run, Pallas kernels for 0% -> 0%
where the time goes in v2:
time: 49.4 us; the launch traced here: 49.2 us
  Pallas kernels  44.6 us (90%)
  local copies, waits for them, and re-layouts  3.82 us (8%)
  between operations  0.73 us (1%)
    pallas_call x1, Pallas kernels, owner_part(): pl.pallas_call(functools.partial(owner_kernel, n), name='owner_sums', out...  21.7 us
    pallas_call x1, Pallas kernels, local_part(): pl.pallas_call(local_kernel, name='mix_and_remap', out_shape=(jax.ShapeDt...  15.9 us
    pallas_call x1, Pallas kernels, halo_part(): pl.pallas_call(functools.partial(halo_kernel, n), name='halo_rows', out_s...  7.05 us
    unnamed x19, local copies, waits for them, and re-layouts  3.82 us

profile of v2, /device:TPU:0, one launch (start us, length us, event | category | flops | bytes accessed | tf_op | source)
XLA Modules:
  0.0 49.2 jit_solution(14449193707326029642)
XLA Ops:
  0.6 0.0 copy-start.6
  0.6 0.0 copy-start.8
  0.7 0.0 copy-start
  0.7 1.4 %copy-done = f32[2,6,8,3600]{3,2,1,0:T(8,128)S(1)} copy-done((f32[2,6,8,3600]{3,2,1,0:T(8,128)S(1)}, f32[2,6,8,3600]{3,2,1,0:T(8,128)}, u32[]{:S(2)}) %copy-start) | copy-done | bytes 1382424
  2.0 0.0 copy-start.2
  2.0 0.9 %copy-done.2 = f32[8,3600]{1,0:T(8,128)S(1)} copy-done((f32[8,3600]{1,0:T(8,128)S(1)}, f32[8,3600]{1,0:T(8,128)}, u32[]{:S(2)}) %copy-start.2) | copy-done | bytes 115224
  2.9 0.0 copy-start.4
  2.9 0.9 %copy-done.4 = s32[8,3600]{1,0:T(8,128)S(1)} copy-done((s32[8,3600]{1,0:T(8,128)S(1)}, s32[8,3600]{1,0:T(8,128)}, u32[]{:S(2)}) %copy-start.4) | copy-done | bytes 115224
  3.8 0.0 copy-start.1
  3.8 0.0 copy-start.3
  3.8 0.0 copy-start.5
  3.8 0.0 copy-start.7
  3.8 7.0 %halo_rows.1 = (f32[2,6,8,3600]{3,2,1,0:T(8,128)S(1)}, f32[8,3600]{1,0:T(8,128)S(1)}, s32[8,3600]{1,0:T(8,128)S(1)}) custom-call(f32[2,6,8,3600]{3,2,1,0:T(8,128)S(1)} %copy-done, f32[8,3600]{1,0:T(8,128)S(1)} %copy-done.2, s32[8,3600]{1,0:T(8,128)S(1)} %copy-done.4), custom_call_target="tpu_custom_call" | custom-call | tf_op jit(solution)/shard_map/halo_rows/pallas_call | solution.py:292
  10.9 0.0 copy-done.6
  10.9 0.0 copy-done.8
  10.9 0.0 copy-done.1
  10.9 0.0 copy-done.3
  10.9 0.0 copy-done.5
  10.9 0.0 copy-done.7
  10.9 15.9 %mix_and_remap.1 = (f32[2,6,8,3600]{3,2,1,0:T(8,128)}, f32[16,13,8,128]{3,2,1,0:T(8,128)S(1)}) custom-call(f32[2,6,8,3600]{3,2,1,0:T(8,128)S(1)} %copy-done.1, f32[8,3600]{1,0:T(8,128)S(1)} %copy-done.3, s32[8,3600]{1,0:T(8,128)S(1)} %copy-done.4, f32[2,6,8,3600]{3,2,1,0:T(8,128)S(1)} %get-tuple-element.7.halo_u, f32[8,3600]{1,0:T(8,128)S(1)} %get-tuple-element.8.halo_kap, ...), custom_call_target="tpu_custom_call" | custom-call | tf_op jit(solution)/shard_map/mix_and_remap/pallas_call | solution.py:311
  26.9 21.7 %owner_sums.1 = f32[12,1024]{1,0:T(8,128)S(1)} custom-call(f32[2,2,4,13,8,128]{5,4,3,2,1,0:T(8,128)S(1)} %bitcast.2), custom_call_target="tpu_custom_call" | custom-call | tf_op jit(solution)/shard_map/owner_sums/pallas_call | solution.py:405
  48.6 0.6 %copy.11 = f32[12,1024]{1,0:T(8,128)} copy(f32[12,1024]{1,0:T(8,128)S(1)} %owner_sums.1) | data formatting | bytes 98304
Async XLA Ops:
  0.6 10.3 %copy-start.6 = (s32[225,1]{0,1:T(1,128)S(1)}, s32[225,1]{0,1:T(1,128)}, u32[]{:S(2)}) copy-start(s32[225,1]{0,1:T(1,128)} %param.13) | copy-start | bytes 2704
  0.6 10.3 %copy-start.8 = (f32[6]{0:T(128)S(1)}, f32[6]{0:T(128)}, u32[]{:S(2)}) copy-start(f32[6]{0:T(128)} %kv_ref.1) | copy-start | bytes 76
  0.7 1.4 %copy-start = (f32[2,6,8,3600]{3,2,1,0:T(8,128)S(1)}, f32[2,6,8,3600]{3,2,1,0:T(8,128)}, u32[]{:S(2)}) copy-start(f32[2,6,8,3600]{3,2,1,0:T(8,128)} %u_ref.1) | copy-start | bytes 4147204
  2.0 0.9 %copy-start.2 = (f32[8,3600]{1,0:T(8,128)S(1)}, f32[8,3600]{1,0:T(8,128)}, u32[]{:S(2)}) copy-start(f32[8,3600]{1,0:T(8,128)} %kap_ref.1) | copy-start | bytes 345604
  2.9 0.9 %copy-start.4 = (s32[8,3600]{1,0:T(8,128)S(1)}, s32[8,3600]{1,0:T(8,128)}, u32[]{:S(2)}) copy-start(s32[8,3600]{1,0:T(8,128)} %wet_ref.1) | copy-start | bytes 345604
  3.8 7.1 %copy-start.1 = (f32[2,6,8,3600]{3,2,1,0:T(8,128)S(1)}, f32[2,6,8,3600]{3,2,1,0:T(8,128)}, u32[]{:S(2)}) copy-start(f32[2,6,8,3600]{3,2,1,0:T(8,128)} %u_ref.1) | copy-start | bytes 4147204
  3.8 7.1 %copy-start.3 = (f32[8,3600]{1,0:T(8,128)S(1)}, f32[8,3600]{1,0:T(8,128)}, u32[]{:S(2)}) copy-start(f32[8,3600]{1,0:T(8,128)} %kap_ref.1) | copy-start | bytes 345604
  3.8 7.1 %copy-start.5 = (f32[12,12]{1,0:T(8,128)S(1)}, f32[12,12]{1,0:T(8,128)}, u32[]{:S(2)}) copy-start(f32[12,12]{1,0:T(8,128)} %coup_ref.1) | copy-start | bytes 1732
  3.8 7.1 %copy-start.7 = (s32[225]{0:T(256)S(1)}, s32[225]{0:T(256)}, u32[]{:S(2)}) copy-start(s32[225]{0:T(256)} %tile_ref.1) | copy-start | bytes 2704

commit v3 on v1

--- a/solution.py
+++ b/solution.py
@@ -24,20 +24,37 @@
     return east, west
 
 
-def row_pair(cur, other, sub):
-    up = pltpu.roll(jnp.where(sub == ROWS - 1, other, cur), 1, 0)
-    down = pltpu.roll(jnp.where(sub == 0, other, cur), ROWS - 1, 0)
-    return up, down
-
-
-def faces(kap, wet, other_kap, other_wet, lane, sub):
-    cur, wcur = kap[0], wet[0]
-    nbk = lane_pair(*kap, lane) + row_pair(cur, other_kap, sub)
-    nbw = lane_pair(*wet, lane) + row_pair(wcur, other_wet, sub)
-    return [(jnp.sqrt(cur * k), jnp.minimum(wcur, w)) for k, w in zip(nbk, nbw)]
-
-
-def mixed(tiles, others, face, wet, kv, lane, sub):
+def row_pair(cur):
+    return pltpu.roll(cur, 1, 0), pltpu.roll(cur, ROWS - 1, 0)
+
+
+def faces(kap, wet, lane, sub, closed):
+    nbk = lane_pair(*kap, lane) + row_pair(kap[0])
+    nbw = lane_pair(*wet, lane) + row_pair(wet[0])
+    depth = [jnp.minimum(wet[0], w) for w in nbw]
+    if closed:
+        depth[2] = jnp.where(sub == 0, 0.0, depth[2])
+        depth[3] = jnp.where(sub == ROWS - 1, 0.0, depth[3])
+    return [(jnp.sqrt(kap[0] * k), d) for k, d in zip(nbk, depth)]
+
+
+def seam_face(kap, wet, halo_kap, halo_wet, sub):
+    edge = (sub == 0) | (sub == ROWS - 1)
+    root = jnp.sqrt(kap * seam(halo_kap, sub))
+    return root, jnp.where(edge, jnp.minimum(wet, seam(halo_wet, sub)), 0.0)
+
+
+def seam(halo, sub):
+    up, down = row_pair(halo)
+    return jnp.where(sub == 0, up, down)
+
+
+def halves(x):
+    hi = x.astype(jnp.bfloat16)
+    return hi, (x - hi.astype(jnp.float32)).astype(jnp.bfloat16)
+
+
+def mixed(tiles, face, wet, kv):
     out = [[None] * NZ for _ in range(2)]
     for l in range(NZ):
         coef = [jnp.where(l < depth, root, 0.0) for root, depth in face]
@@ -45,9 +62,8 @@
         above = jnp.where(l < wet, kv[l - 1], 0.0) if l > 0 else None
         for c in range(2):
             cur = tiles[c][l][0]
-            near = lane_pair(*tiles[c][l], lane) + row_pair(cur, others[c][l], sub)
-            change = coef[0] * (near[0] - cur)
-            for a, v in zip(coef[1:], near[1:]):
+            change = coef[0] * (tiles[c][l][1] - cur)
+            for a, v in zip(coef[1:], tiles[c][l][2:]):
                 change = change + a * (v - cur)
             if below is not None:
                 change = change + below * (tiles[c][l + 1][0] - cur)
@@ -57,26 +73,94 @@
     return out
 
 
-def local_kernel(
-    u_ref, kap_ref, wet_ref, halo_ref, kv_ref, coup_ref, dest_ref, tile_ref, w_hbm,
-    next_ref, sums_ref,
-    full, mid, surf, blocks, acc, weights, w_sem,
-):
+def columns(t, tiles):
+    def at(i):
+        return pl.ds(pl.multiple_of(i * LANES, LANES), LANES)
+
+    return [at(t), at(lax.rem(t + tiles - 1, tiles)), at(lax.rem(t + 1, tiles))]
+
+
+def closed_step(src, full, dst, kv, lane, sub, tiles):
+    def one(t, carry):
+        cols = columns(t, tiles)
+        get = lambda ref, q: [ref[0, q, :, s] for s in cols]
+        state = []
+        for c in range(2):
+            state.append([])
+            for l in range(NZ):
+                cur = get(src, c * NZ + l)
+                state[c].append((cur[0],) + lane_pair(*cur, lane) + row_pair(cur[0]))
+        wet = get(full, 12 + 1)
+        face = faces(get(full, 12), wet, lane, sub, True)
+        new = mixed(state, face, wet[0], kv)
+        for c in range(2):
+            for l in range(NZ):
+                dst[0, c * NZ + l, :, cols[0]] = new[c][l]
+        return carry
+
+    lax.fori_loop(0, tiles, one, 0)
+
+
+def add_seam(value, band, halo, face, l, sub):
+    coef = jnp.where(l < face[1], face[0], 0.0)
+    return value + coef * (seam(halo, sub) - band)
+
+
+def step_kernel(n, u_ref, kap_ref, wet_ref, kv_ref, full, mid, nxt, *refs):
+    outgoing, incoming, send, recv = refs
+    me = lax.axis_index("blk")
+    incoming[...] = jnp.zeros_like(incoming)
+    barrier = pltpu.get_barrier_semaphore()
+    for other in (lax.rem(me + n - 1, n), lax.rem(me + 1, n)):
+        pl.semaphore_signal(
+            barrier, inc=1, device_id={"blk": other}, device_id_type=pl.DeviceIdType.MESH
+        )
+
     length = u_ref.shape[-1]
-    count = w_hbm.shape[0]
     tiles = full.shape[-1] // LANES
     last = tiles - 1
     rem = length - last * LANES
     cut = last * LANES
-    fetch = pltpu.make_async_copy(w_hbm, weights, w_sem)
-    fetch.start()
-
     lane = lax.broadcasted_iota(jnp.int32, (ROWS, LANES), 1)
     sub = lax.broadcasted_iota(jnp.int32, (ROWS, LANES), 0)
     kv = [kv_ref[l] for l in range(NZ)]
 
-    def place(side, q, value):
-        full[side, q, :, 0:cut] = value[:, 0:cut]
+    sides = [(me > 0, me - 1), (me < n - 1, me + 1)]
+
+    def edge_row(far, i):
+        row = (far, ROWS - 1 - far)[i]
+        return slice(row, row + 1)
+
+    def copies(far, i):
+        return [pltpu.make_async_remote_copy(
+            src_ref=outgoing.at[far, i], dst_ref=incoming.at[far, i],
+            send_sem=send.at[far, i], recv_sem=recv.at[far, i],
+            device_id={"blk": sides[i][1]}, device_id_type=pl.DeviceIdType.MESH,
+        )]
+
+    def start(far):
+        for i in range(2):
+            for q in range(14):
+                outgoing[far, i, q:q + 1, :] = full[0, q, edge_row(far, i), :]
+            @pl.when(sides[i][0])
+            def _():
+                for one in copies(far, i):
+                    one.start()
+
+    def arrive(far):
+        for i in range(2):
+            @pl.when(sides[1 - i][0])
+            def _():
+                for one in copies(far, i):
+                    one.wait_recv()
+
+    def spread_out(far):
+        for i in range(2):
+            for q in range(14):
+                full[1, q, edge_row(far, i), :] = incoming[far, i, q:q + 1, :]
+
+    def place(q, value):
+        full[0, q, :, 0:cut] = value[:, 0:cut]
         tail = jnp.concatenate(
             [value[:, cut:length], jnp.zeros((ROWS, LANES - rem), jnp.float32)], axis=1
         )
@@ -90,40 +174,102 @@
                 pltpu.roll(tail, LANES - rem, 1),
             ),
         )
-        full[side, q, :, cut:] = tail
+        full[0, q, :, cut:] = tail
 
     for c in range(2):
         for l in range(NZ):
-            place(0, c * NZ + l, u_ref[c, l])
-    place(0, 12, kap_ref[...])
-    place(0, 13, wet_ref[...].astype(jnp.float32))
-    for q in range(14):
-        place(1, q, halo_ref[q])
+            place(c * NZ + l, u_ref[c, l])
+    place(12, kap_ref[...])
+    place(13, wet_ref[...].astype(jnp.float32))
+    full[1] = jnp.zeros(full.shape[1:], jnp.float32)
+    outgoing[...] = jnp.zeros_like(outgoing)
+    pl.semaphore_wait(barrier, 2)
+    start(0)
+    closed_step(full, full, mid, kv, lane, sub, tiles)
+    start(1)
+    arrive(0)
+    spread_out(0)
+
+    def near(t, carry):
+        here = columns(t, tiles)[0]
+        face = seam_face(
+            full[0, 12, :, here], full[0, 13, :, here], full[1, 12, :, here], full[1, 13, :, here], sub
+        )
+        for q in range(2 * NZ):
+            mid[0, q, :, here] = add_seam(
+                mid[0, q, :, here], full[0, q, :, here], full[1, q, :, here], face, q % NZ, sub
+            )
+        return carry
+
+    lax.fori_loop(0, tiles, near, 0)
+    closed_step(mid, full, nxt, kv, lane, sub, tiles)
+    arrive(1)
+    spread_out(1)
+
+    def halo_step(t, carry):
+        cols = columns(t, tiles)
+
+        def get(q):
+            cur = [full[1, q, :, s] for s in cols]
+            band = full[0, q, :, cols[0]]
+            up = pltpu.roll(jnp.where(sub == ROWS - 1, band, cur[0]), 1, 0)
+            down = pltpu.roll(jnp.where(sub == 0, band, cur[0]), ROWS - 1, 0)
+            return (cur[0],) + lane_pair(*cur, lane) + (up, down)
+
+        state = [[get(c * NZ + l) for l in range(NZ)] for c in range(2)]
+        kap, wet = get(12), get(13)
+        face = [(jnp.sqrt(kap[0] * k), jnp.minimum(wet[0], w)) for k, w in zip(kap[1:], wet[1:])]
+        new = mixed(state, face, wet[0], kv)
+        for c in range(2):
+            for l in range(NZ):
+                mid[1, c * NZ + l, :, cols[0]] = new[c][l]
+        return carry
+
+    lax.fori_loop(0, tiles, halo_step, 0)
+    for far in range(2):
+        for i in range(2):
+            @pl.when(sides[i][0])
+            def _():
+                for one in copies(far, i):
+                    one.wait_send()
+
+
+def step_part(u, kap, wet, kv, n):
+    pad = -(-u.shape[-1] // LANES) * LANES
+    vmem = pl.BlockSpec(memory_space=pltpu.VMEM)
+    smem = pl.BlockSpec(memory_space=pltpu.SMEM)
+    return pl.pallas_call(
+        functools.partial(step_kernel, n),
+        name="two_steps",
+        out_shape=tuple(
+            jax.ShapeDtypeStruct(x + (ROWS, pad), jnp.float32) for x in ((2, 14), (2, 12), (1, 12))
+        ),
+        in_specs=[vmem] * 3 + [smem],
+        out_specs=(vmem,) * 3,
+        scratch_shapes=[pltpu.VMEM((2, 2, 16, pad), jnp.float32)] * 2
+        + [pltpu.SemaphoreType.DMA((2, 2))] * 2,
+        compiler_params=pltpu.CompilerParams(
+            collective_id=1, has_side_effects=True, vmem_limit_bytes=24 * 2**20
+        ),
+    )(u, kap, wet, kv)
+
+
+def local_kernel(
+    full, mid, nxt, coup_ref, dest_ref, tile_ref, w_hbm,
+    next_ref, sums_ref,
+    surf, blocks, acc, weights, w_sem,
+):
+    length = next_ref.shape[-1]
+    count = w_hbm.shape[0]
+    tiles = full.shape[-1] // LANES
+    last = tiles - 1
+    rem = length - last * LANES
+    cut = last * LANES
+    fetch = pltpu.make_async_copy(w_hbm, weights, w_sem)
+    fetch.start()
+
+    sub = lax.broadcasted_iota(jnp.int32, (ROWS, LANES), 0)
     acc[...] = jnp.zeros_like(acc)
-
-    def columns(t):
-        def at(i):
-            return pl.ds(pl.multiple_of(i * LANES, LANES), LANES)
-
-        return [at(t), at(lax.rem(t + last, tiles)), at(lax.rem(t + 1, tiles))]
-
-    def first(t, carry):
-        cols = columns(t)
-        get = lambda side, q: [full[side, q, :, s] for s in cols]
-        state = [[[get(side, c * NZ + l) for l in range(NZ)] for c in range(2)] for side in range(2)]
-        kap = [get(side, 12) for side in range(2)]
-        wet = [get(side, 13) for side in range(2)]
-        for side in range(2):
-            o = 1 - side
-            face = faces(kap[side], wet[side], kap[o][0], wet[o][0], lane, sub)
-            others = [[state[o][c][l][0] for l in range(NZ)] for c in range(2)]
-            new = mixed(state[side], others, face, wet[side][0], kv, lane, sub)
-            for c in range(2):
-                for l in range(NZ):
-                    mid[side, c * NZ + l, :, cols[0]] = new[c][l]
-        return carry
-
-    lax.fori_loop(0, tiles, first, 0)
 
     big = ROWS * WIDE
     inner = (FIELDS + 1) * ROWS
@@ -142,32 +288,43 @@
     same = (m0 // WIDE) == lax.rem(m1, ROWS)
     sea_entry = (lax.rem(m0, WIDE) == FIELDS) & (m1 // ROWS == FIELDS)
     spread = jnp.where(same, jnp.where(sea_entry, 1.0, spread), 0.0)
+    spread_hi, spread_lo = halves(spread)
+    spread3 = jnp.concatenate([spread_hi, spread_hi, spread_lo], axis=1)
 
     def second(t):
-        cols = columns(t)
-        get = lambda ref, side, q: [ref[side, q, :, s] for s in cols]
-        state = [[get(mid, 0, c * NZ + l) for l in range(NZ)] for c in range(2)]
-        others = [[mid[1, c * NZ + l, :, cols[0]] for l in range(NZ)] for c in range(2)]
-        kap, wet = get(full, 0, 12), get(full, 0, 13)
-        face = faces(kap, wet, full[1, 12, :, cols[0]], full[1, 13, :, cols[0]], lane, sub)
-        new = mixed(state, others, face, wet[0], kv, lane, sub)
-        sea = jnp.where(wet[0] > 0.0, 1.0, 0.0)
+        here = columns(t, tiles)[0]
+        wet = full[0, 13, :, here]
+        face = seam_face(full[0, 12, :, here], wet, full[1, 12, :, here], full[1, 13, :, here], sub)
+        new = [
+            add_seam(nxt[0, q, :, here], mid[0, q, :, here], mid[1, q, :, here], face, q % NZ, sub)
+            for q in range(2 * NZ)
+        ]
+        new = [new[:NZ], new[NZ:]]
+        sea = jnp.where(wet > 0.0, 1.0, 0.0)
         rows = [new[c][l] * sea for c in range(2) for l in range(NZ)] + [sea]
-        surf[:, cols[0]] = jnp.dot(
-            spread, jnp.concatenate(rows, axis=0), precision=HIGH,
-            preferred_element_type=jnp.float32,
-        )
-        return new, cols[0]
-
-    def second_loop(t, carry):
-        new, here = second(t)
-        for c in range(2):
-            for l in range(NZ):
-                next_ref[c, l, :, here] = new[c][l]
-        return carry
-
-    lax.fori_loop(0, last, second_loop, 0)
-    new, _ = second(last)
+        return new, here, jnp.concatenate(rows, axis=0)
+
+    def couple(profile):
+        hi, lo = halves(profile)
+        return jnp.dot(
+            spread3, jnp.concatenate([hi, lo, hi], axis=0), preferred_element_type=jnp.float32
+        )
+
+    def second_loop(p, carry):
+        profiles = []
+        for k in range(2):
+            new, here, profile = second(2 * p + k)
+            profiles.append(profile)
+            for c in range(2):
+                for l in range(NZ):
+                    next_ref[c, l, :, here] = new[c][l]
+        here = pl.ds(pl.multiple_of(p * (2 * LANES), LANES), 2 * LANES)
+        surf[:, here] = couple(jnp.concatenate(profiles, axis=1))
+        return carry
+
+    lax.fori_loop(0, last // 2, second_loop, 0)
+    new, here, profile = second(last)
+    surf[:, here] = couple(profile)
     for c in range(2):
         for l in range(NZ):
             next_ref[c, l, :, cut:length] = new[c][l][:, 0:rem]
@@ -189,7 +346,7 @@
             blocks[last * j + t] = value.astype(jnp.bfloat16)
         return carry
 
-    lax.fori_loop(1, last, align, 0)
+    lax.fori_loop(1, last, align, 0, unroll=3)
     for j in range(ROWS + 1):
         if j > 0:
             rows = pl.ds((j - 1) * WIDE, WIDE)
@@ -211,7 +368,7 @@
         acc[here, :] = acc[here, :] + value
         return carry
 
-    lax.fori_loop(0, count, product, 0, unroll=9)
+    lax.fori_loop(0, count, product, 0, unroll=25)
 
     owners = sums_ref.shape[0]
     quarter = owners // 4
@@ -226,24 +383,21 @@
     lax.fori_loop(0, owners, deliver, 0)
 
 
-def local_part(u, kap, wet, halo, kv, coup, dest, tile, weights, owners):
-    length = u.shape[-1]
-    pad = -(-length // LANES) * LANES
+def local_part(full, mid, nxt, coup, dest, tile, weights, length, owners):
+    pad = full.shape[-1]
     count = weights.shape[0]
     vmem = pl.BlockSpec(memory_space=pltpu.VMEM)
     smem = pl.BlockSpec(memory_space=pltpu.SMEM)
     return pl.pallas_call(
         local_kernel,
-        name="mix_and_remap",
+        name="remap",
         out_shape=(
-            jax.ShapeDtypeStruct(u.shape, jnp.float32),
+            jax.ShapeDtypeStruct((2, NZ, ROWS, length), jnp.float32),
             jax.ShapeDtypeStruct((owners, FIELDS + 1, NTILE, AT), jnp.float32),
         ),
-        in_specs=[vmem, vmem, vmem, vmem, smem, vmem, smem, smem, pl.BlockSpec(memory_space=pl.ANY)],
+        in_specs=[vmem] * 4 + [smem, smem, pl.BlockSpec(memory_space=pl.ANY)],
         out_specs=(vmem, vmem),
         scratch_shapes=[
-            pltpu.VMEM((2, 14, ROWS, pad), jnp.float32),
-            pltpu.VMEM((2, 12, ROWS, pad), jnp.float32),
             pltpu.VMEM((ROWS * WIDE, pad), jnp.float32),
             pltpu.VMEM((count, WIDE, CB), jnp.bfloat16),
             pltpu.VMEM((owners * NTILE * WIDE, AT), jnp.float32),
@@ -251,10 +405,10 @@
             pltpu.SemaphoreType.DMA,
         ],
         compiler_params=pltpu.CompilerParams(vmem_limit_bytes=44 * 2**20),
-    )(u, kap, wet, halo, kv, coup, dest, tile, weights)
-
-
-PARTS = ((0, 7), (7, 13))
+    )(full, mid, nxt, coup, dest, tile, weights)
+
+
+PARTS = ((0, 4), (4, 7), (7, 10), (10, 13))
 
 
 def owner_kernel(n, sums_ref, out_ref, sum1, sum2, got1, got2, got3, ratio, send, recv):
@@ -352,24 +506,10 @@
     ocean_state, kappa_h, kappa_v, wet_depth, coupling, dest_of_block, tile_of_block, remap_weights
 ):
     size = lax.axis_size("blk")
-    length = ocean_state.shape[-1]
-    stacked = jnp.concatenate(
-        [
-            ocean_state.reshape(2 * NZ, ROWS, length),
-            kappa_h[None],
-            wet_depth.astype(jnp.float32)[None],
-        ],
-        axis=0,
-    )
-    up = [(i, i + 1) for i in range(size - 1)]
-    down = [(i + 1, i) for i in range(size - 1)]
-    before = lax.ppermute(stacked[:, ROWS - 2:], "blk", up)
-    after = lax.ppermute(stacked[:, :2], "blk", down)
-    zeros = jnp.zeros((2 * NZ + 2, ROWS - 4, length), jnp.float32)
-    halo = jnp.concatenate([after, zeros, before], axis=1)
+    steps = step_part(ocean_state, kappa_h, wet_depth, kappa_v, size)
     ocean_next, sums = local_part(
-        ocean_state, kappa_h, wet_depth, halo, kappa_v, coupling,
-        dest_of_block.reshape(-1), tile_of_block, remap_weights, size,
+        *steps, coupling, dest_of_block.reshape(-1), tile_of_block, remap_weights,
+        ocean_state.shape[-1], size,
     )
     return ocean_next, owner_part(sums)
 

time: 59.3 us -> 52 us (0.88)
  local copies, waits for them, and re-layouts: 0.75 us -> 6.48 us
  starting transfers between devices: 4.48 us -> 0 us
  Pallas kernels: 48.3 us -> 44.6 us
  other arithmetic: 3.51 us -> 0 us
  waiting for transfers between devices: 1.25 us -> 0 us
    pallas_call x1, Pallas kernels: 25.2 us -> 17.8 us  [owner_part(): pl.pallas_call(functools.partial(owner_kernel, n), name='owner_sums', out...]
    unnamed x15, local copies, waits for them, and re-layouts: 0.68 us -> 6.48 us
    ppermute x2 -> x0, starting transfers between devices: 4.48 us -> none  [the longest x1 3.06 us: body(): before = lax.ppermute(stacked[:, ROWS - 2:], 'blk', up)]
    pallas_call x1 -> x2, Pallas kernels: 23.1 us -> 26.8 us  [the longest x1 16.9 us: step_part(): pl.pallas_call(functools.partial(step_kernel, n), name='two_steps', out_s...]
    slice x1 -> x0, other arithmetic: 2.21 us -> none  [body(): after = lax.ppermute(stacked[:, :2], 'blk', down)]
    ppermute x2 -> x0, waiting for transfers between devices: 1.25 us -> none  [the longest x1 1.25 us: body(): before = lax.ppermute(stacked[:, ROWS - 2:], 'blk', up)]
    broadcast_in_dim x1 -> x0, other arithmetic: 0.91 us -> none  [body(): wet_depth.astype(jnp.float32)[None]]
  transfers between devices with their start and end apart: 2 -> 0, of which waited for: 1 -> 0; matrix products, arithmetic and copies ran while one was open for 0% -> 0% of each run, Pallas kernels for 0% -> 0%
where the time goes in v3:
time: 52 us; the launch traced here: 51.8 us
  Pallas kernels  44.6 us (86%)
  local copies, waits for them, and re-layouts  6.48 us (12%)
  between operations  0.68 us (1%)
    pallas_call x1, Pallas kernels, owner_part(): pl.pallas_call(functools.partial(owner_kernel, n), name='owner_sums', out...  17.8 us
    pallas_call x1, Pallas kernels, step_part(): pl.pallas_call(functools.partial(step_kernel, n), name='two_steps', out_s...  16.9 us
    pallas_call x1, Pallas kernels, local_part(): pl.pallas_call(local_kernel, name='remap', out_shape=(jax.ShapeDtypeStruc...  9.82 us
    unnamed x15, local copies, waits for them, and re-layouts  6.48 us

profile of v3, /device:TPU:0, one launch (start us, length us, event | category | flops | bytes accessed | tf_op | source)
XLA Modules:
  0.0 51.8 jit_solution(17868698974694347794)
XLA Ops:
  0.6 0.0 copy-start
  0.6 1.3 %copy-done = f32[2,6,8,3600]{3,2,1,0:T(8,128)S(1)} copy-done((f32[2,6,8,3600]{3,2,1,0:T(8,128)S(1)}, f32[2,6,8,3600]{3,2,1,0:T(8,128)}, u32[]{:S(2)}) %copy-start) | copy-done | bytes 1382424
  2.0 0.0 copy-start.1
  2.0 0.9 %copy-done.1 = f32[8,3600]{1,0:T(8,128)S(1)} copy-done((f32[8,3600]{1,0:T(8,128)S(1)}, f32[8,3600]{1,0:T(8,128)}, u32[]{:S(2)}) %copy-start.1) | copy-done | bytes 115224
  2.9 0.0 copy-start.2
  2.9 0.9 %copy-done.2 = s32[8,3600]{1,0:T(8,128)S(1)} copy-done((s32[8,3600]{1,0:T(8,128)S(1)}, s32[8,3600]{1,0:T(8,128)}, u32[]{:S(2)}) %copy-start.2) | copy-done | bytes 115224
  3.8 0.0 copy-start.6
  3.8 0.7 %copy-done.6 = f32[6]{0:T(128)S(1)} copy-done((f32[6]{0:T(128)S(1)}, f32[6]{0:T(128)}, u32[]{:S(2)}) %copy-start.6) | copy-done | bytes 48
  4.4 16.9 %two_steps.1 = (f32[2,14,8,3712]{3,2,1,0:T(8,128)S(1)}, f32[2,12,8,3712]{3,2,1,0:T(8,128)S(1)}, f32[1,12,8,3712]{3,2,1,0:T(8,128)S(1)}) custom-call(f32[2,6,8,3600]{3,2,1,0:T(8,128)S(1)} %copy-done, f32[8,3600]{1,0:T(8,128)S(1)} %copy-done.1, s32[8,3600]{1,0:T(8,128)S(1)} %copy-done.2, f32[6]{0:T(128)S(1)} %copy-done.6), custom_call_target="tpu_custom_call" | custom-call | tf_op jit(solution)/shard_map/two_steps/pallas_call | solution.py:241
  21.4 0.0 copy-start.3
  21.4 0.7 %copy-done.3 = f32[12,12]{1,0:T(8,128)S(1)} copy-done((f32[12,12]{1,0:T(8,128)S(1)}, f32[12,12]{1,0:T(8,128)}, u32[]{:S(2)}) %copy-start.3) | copy-done | bytes 600
  22.1 0.0 copy-start.4
  22.1 0.7 %copy-done.4 = s32[225,1]{0,1:T(1,128)S(1)} copy-done((s32[225,1]{0,1:T(1,128)S(1)}, s32[225,1]{0,1:T(1,128)}, u32[]{:S(2)}) %copy-start.4) | copy-done | bytes 924
  22.8 0.0 copy-start.5
  22.8 0.7 %copy-done.5 = s32[225]{0:T(256)S(1)} copy-done((s32[225]{0:T(256)S(1)}, s32[225]{0:T(256)}, u32[]{:S(2)}) %copy-start.5) | copy-done | bytes 924
  23.4 9.8 %remap.1 = (f32[2,6,8,3600]{3,2,1,0:T(8,128)}, f32[16,13,8,128]{3,2,1,0:T(8,128)S(1)}) custom-call(f32[2,14,8,3712]{3,2,1,0:T(8,128)S(1)} %get-tuple-element.7.full, f32[2,12,8,3712]{3,2,1,0:T(8,128)S(1)} %get-tuple-element.8.mid, f32[1,12,8,3712]{3,2,1,0:T(8,128)S(1)} %get-tuple-element.9.nxt, f32[12,12]{1,0:T(8,128)S(1)} %copy-done.3, s32[225]{0:T(256)S(1)} %bitcast.3, ...), custom_call_target="tpu_custom_call" | custom-call | tf_op jit(solution)/shard_map/remap/pallas_call | solution.py:391
  33.3 17.8 %owner_sums.1 = f32[12,1024]{1,0:T(8,128)S(1)} custom-call(f32[2,2,4,13,8,128]{5,4,3,2,1,0:T(8,128)S(1)} %bitcast.2), custom_call_target="tpu_custom_call" | custom-call | tf_op jit(solution)/shard_map/owner_sums/pallas_call | solution.py:483
  51.1 0.6 %copy.11 = f32[12,1024]{1,0:T(8,128)} copy(f32[12,1024]{1,0:T(8,128)S(1)} %owner_sums.1) | data formatting | bytes 98304
Async XLA Ops:
  0.6 1.4 %copy-start = (f32[2,6,8,3600]{3,2,1,0:T(8,128)S(1)}, f32[2,6,8,3600]{3,2,1,0:T(8,128)}, u32[]{:S(2)}) copy-start(f32[2,6,8,3600]{3,2,1,0:T(8,128)} %u_ref.1) | copy-start | bytes 4147204
  2.0 0.9 %copy-start.1 = (f32[8,3600]{1,0:T(8,128)S(1)}, f32[8,3600]{1,0:T(8,128)}, u32[]{:S(2)}) copy-start(f32[8,3600]{1,0:T(8,128)} %kap_ref.1) | copy-start | bytes 345604
  2.9 0.9 %copy-start.2 = (s32[8,3600]{1,0:T(8,128)S(1)}, s32[8,3600]{1,0:T(8,128)}, u32[]{:S(2)}) copy-start(s32[8,3600]{1,0:T(8,128)} %wet_ref.1) | copy-start | bytes 345604
  3.8 0.7 %copy-start.6 = (f32[6]{0:T(128)S(1)}, f32[6]{0:T(128)}, u32[]{:S(2)}) copy-start(f32[6]{0:T(128)} %kv_ref.1) | copy-start | bytes 76
  21.4 0.7 %copy-start.3 = (f32[12,12]{1,0:T(8,128)S(1)}, f32[12,12]{1,0:T(8,128)}, u32[]{:S(2)}) copy-start(f32[12,12]{1,0:T(8,128)} %coup_ref.1) | copy-start | bytes 1732
  22.1 0.7 %copy-start.4 = (s32[225,1]{0,1:T(1,128)S(1)}, s32[225,1]{0,1:T(1,128)}, u32[]{:S(2)}) copy-start(s32[225,1]{0,1:T(1,128)} %param.13) | copy-start | bytes 2704
  22.8 0.7 %copy-start.5 = (s32[225]{0:T(256)S(1)}, s32[225]{0:T(256)}, u32[]{:S(2)}) copy-start(s32[225]{0:T(256)} %tile_ref.1) | copy-start | bytes 2704

commit v4 on v3

--- a/solution.py
+++ b/solution.py
@@ -101,9 +101,8 @@
     lax.fori_loop(0, tiles, one, 0)
 
 
-def add_seam(value, band, halo, face, l, sub):
-    coef = jnp.where(l < face[1], face[0], 0.0)
-    return value + coef * (seam(halo, sub) - band)
+def seam_coef(face, l):
+    return jnp.where(l < face[1], face[0], 0.0)
 
 
 def step_kernel(n, u_ref, kap_ref, wet_ref, kv_ref, full, mid, nxt, *refs):
@@ -127,8 +126,8 @@
 
     sides = [(me > 0, me - 1), (me < n - 1, me + 1)]
 
-    def edge_row(far, i):
-        row = (far, ROWS - 1 - far)[i]
+    def edge_row(i):
+        row = (0, ROWS - 1)[i]
         return slice(row, row + 1)
 
     def copies(far, i):
@@ -138,10 +137,11 @@
             device_id={"blk": sides[i][1]}, device_id_type=pl.DeviceIdType.MESH,
         )]
 
-    def start(far):
+    def start(far, source, rows):
         for i in range(2):
-            for q in range(14):
-                outgoing[far, i, q:q + 1, :] = full[0, q, edge_row(far, i), :]
+            for q in range(rows):
+                outgoing[far, i, q:q + 1, :] = source[0, q, edge_row(i), :]
+
             @pl.when(sides[i][0])
             def _():
                 for one in copies(far, i):
@@ -154,10 +154,10 @@
                 for one in copies(far, i):
                     one.wait_recv()
 
-    def spread_out(far):
+    def spread_out(far, target, rows):
         for i in range(2):
-            for q in range(14):
-                full[1, q, edge_row(far, i), :] = incoming[far, i, q:q + 1, :]
+            for q in range(rows):
+                target[1, q, edge_row(i), :] = incoming[far, i, q:q + 1, :]
 
     def place(q, value):
         full[0, q, :, 0:cut] = value[:, 0:cut]
@@ -184,11 +184,12 @@
     full[1] = jnp.zeros(full.shape[1:], jnp.float32)
     outgoing[...] = jnp.zeros_like(outgoing)
     pl.semaphore_wait(barrier, 2)
-    start(0)
+    start(0, full, 14)
     closed_step(full, full, mid, kv, lane, sub, tiles)
-    start(1)
+    start(1, mid, 2 * NZ)
+    mid[1] = jnp.zeros(mid.shape[1:], jnp.float32)
     arrive(0)
-    spread_out(0)
+    spread_out(0, full, 14)
 
     def near(t, carry):
         here = columns(t, tiles)[0]
@@ -196,36 +197,14 @@
             full[0, 12, :, here], full[0, 13, :, here], full[1, 12, :, here], full[1, 13, :, here], sub
         )
         for q in range(2 * NZ):
-            mid[0, q, :, here] = add_seam(
-                mid[0, q, :, here], full[0, q, :, here], full[1, q, :, here], face, q % NZ, sub
-            )
+            flux = seam_coef(face, q % NZ) * (seam(full[1, q, :, here], sub) - full[0, q, :, here])
+            mid[0, q, :, here] = mid[0, q, :, here] + flux
         return carry
 
     lax.fori_loop(0, tiles, near, 0)
     closed_step(mid, full, nxt, kv, lane, sub, tiles)
     arrive(1)
-    spread_out(1)
-
-    def halo_step(t, carry):
-        cols = columns(t, tiles)
-
-        def get(q):
-            cur = [full[1, q, :, s] for s in cols]
-            band = full[0, q, :, cols[0]]
-            up = pltpu.roll(jnp.where(sub == ROWS - 1, band, cur[0]), 1, 0)
-            down = pltpu.roll(jnp.where(sub == 0, band, cur[0]), ROWS - 1, 0)
-            return (cur[0],) + lane_pair(*cur, lane) + (up, down)
-
-        state = [[get(c * NZ + l) for l in range(NZ)] for c in range(2)]
-        kap, wet = get(12), get(13)
-        face = [(jnp.sqrt(kap[0] * k), jnp.minimum(wet[0], w)) for k, w in zip(kap[1:], wet[1:])]
-        new = mixed(state, face, wet[0], kv)
-        for c in range(2):
-            for l in range(NZ):
-                mid[1, c * NZ + l, :, cols[0]] = new[c][l]
-        return carry
-
-    lax.fori_loop(0, tiles, halo_step, 0)
+    spread_out(1, mid, 2 * NZ)
     for far in range(2):
         for i in range(2):
             @pl.when(sides[i][0])
@@ -241,6 +220,7 @@
     return pl.pallas_call(
         functools.partial(step_kernel, n),
         name="two_steps",
+        cost_estimate=pl.CostEstimate(flops=20000000, bytes_accessed=12000000, transcendentals=0),
         out_shape=tuple(
             jax.ShapeDtypeStruct(x + (ROWS, pad), jnp.float32) for x in ((2, 14), (2, 12), (1, 12))
         ),
@@ -295,10 +275,12 @@
         here = columns(t, tiles)[0]
         wet = full[0, 13, :, here]
         face = seam_face(full[0, 12, :, here], wet, full[1, 12, :, here], full[1, 13, :, here], sub)
-        new = [
-            add_seam(nxt[0, q, :, here], mid[0, q, :, here], mid[1, q, :, here], face, q % NZ, sub)
-            for q in range(2 * NZ)
-        ]
+        new = []
+        for q in range(2 * NZ):
+            coef = seam_coef(face, q % NZ)
+            flux = coef * (seam(full[1, q, :, here], sub) - full[0, q, :, here])
+            beyond = seam(mid[1, q, :, here], sub) - flux
+            new.append(nxt[0, q, :, here] + coef * (beyond - mid[0, q, :, here]))
         new = [new[:NZ], new[NZ:]]
         sea = jnp.where(wet > 0.0, 1.0, 0.0)
         rows = [new[c][l] * sea for c in range(2) for l in range(NZ)] + [sea]
@@ -391,6 +373,7 @@
     return pl.pallas_call(
         local_kernel,
         name="remap",
+        cost_estimate=pl.CostEstimate(flops=200000000, bytes_accessed=18000000, transcendentals=0),
         out_shape=(
             jax.ShapeDtypeStruct((2, NZ, ROWS, length), jnp.float32),
             jax.ShapeDtypeStruct((owners, FIELDS + 1, NTILE, AT), jnp.float32),
@@ -483,6 +466,7 @@
     return pl.pallas_call(
         functools.partial(owner_kernel, n),
         name="owner_sums",
+        cost_estimate=pl.CostEstimate(flops=1000000, bytes_accessed=4000000, transcendentals=0),
         out_shape=jax.ShapeDtypeStruct((FIELDS, NTILE * AT), jnp.float32),
         in_specs=[vmem],
         out_specs=vmem,

time: 52 us -> 49 us (0.942)
  Pallas kernels: 44.6 us -> 41.6 us
    pallas_call x3, Pallas kernels: 44.6 us -> 41.6 us  [the longest x1 17.8 us: owner_part(): pl.pallas_call(functools.partial(owner_kernel, n), name='owner_sums', cos...]
where the time goes in v4:
time: 49 us; the launch traced here: 48.8 us
  Pallas kernels  41.6 us (85%)
  local copies, waits for them, and re-layouts  6.48 us (13%)
  between operations  0.68 us (1%)
    pallas_call x1, Pallas kernels, owner_part(): pl.pallas_call(functools.partial(owner_kernel, n), name='owner_sums', cos...  17.8 us
    pallas_call x1, Pallas kernels, step_part(): pl.pallas_call(functools.partial(step_kernel, n), name='two_steps', cost_...  13.7 us
    pallas_call x1, Pallas kernels, local_part(): pl.pallas_call(local_kernel, name='remap', cost_estimate=pl.CostEstimate(...  10.1 us
    unnamed x15, local copies, waits for them, and re-layouts  6.48 us

profile of v4, /device:TPU:0, one launch (start us, length us, event | category | flops | bytes accessed | tf_op | source)
XLA Modules:
  0.0 48.8 jit_solution(15732885840992773061)
XLA Ops:
  0.6 0.0 copy-start
  0.6 1.3 %copy-done = f32[2,6,8,3600]{3,2,1,0:T(8,128)S(1)} copy-done((f32[2,6,8,3600]{3,2,1,0:T(8,128)S(1)}, f32[2,6,8,3600]{3,2,1,0:T(8,128)}, u32[]{:S(2)}) %copy-start) | copy-done | bytes 1382424
  2.0 0.0 copy-start.1
  2.0 0.9 %copy-done.1 = f32[8,3600]{1,0:T(8,128)S(1)} copy-done((f32[8,3600]{1,0:T(8,128)S(1)}, f32[8,3600]{1,0:T(8,128)}, u32[]{:S(2)}) %copy-start.1) | copy-done | bytes 115224
  2.9 0.0 copy-start.2
  2.9 0.9 %copy-done.2 = s32[8,3600]{1,0:T(8,128)S(1)} copy-done((s32[8,3600]{1,0:T(8,128)S(1)}, s32[8,3600]{1,0:T(8,128)}, u32[]{:S(2)}) %copy-start.2) | copy-done | bytes 115224
  3.8 0.0 copy-start.6
  3.8 0.7 %copy-done.6 = f32[6]{0:T(128)S(1)} copy-done((f32[6]{0:T(128)S(1)}, f32[6]{0:T(128)}, u32[]{:S(2)}) %copy-start.6) | copy-done | bytes 48
  4.4 13.7 %two_steps.1 = (f32[2,14,8,3712]{3,2,1,0:T(8,128)S(1)}, f32[2,12,8,3712]{3,2,1,0:T(8,128)S(1)}, f32[1,12,8,3712]{3,2,1,0:T(8,128)S(1)}) custom-call(f32[2,6,8,3600]{3,2,1,0:T(8,128)S(1)} %copy-done, f32[8,3600]{1,0:T(8,128)S(1)} %copy-done.1, s32[8,3600]{1,0:T(8,128)S(1)} %copy-done.2, f32[6]{0:T(128)S(1)} %copy-done.6), custom_call_target="tpu_custom_call" | custom-call | flops 20000000 | bytes 12000000 | tf_op jit(solution)/shard_map/two_steps/pallas_call | solution.py:220
  18.2 0.0 copy-start.3
  18.2 0.7 %copy-done.3 = f32[12,12]{1,0:T(8,128)S(1)} copy-done((f32[12,12]{1,0:T(8,128)S(1)}, f32[12,12]{1,0:T(8,128)}, u32[]{:S(2)}) %copy-start.3) | copy-done | bytes 600
  18.9 0.0 copy-start.4
  18.9 0.7 %copy-done.4 = s32[225,1]{0,1:T(1,128)S(1)} copy-done((s32[225,1]{0,1:T(1,128)S(1)}, s32[225,1]{0,1:T(1,128)}, u32[]{:S(2)}) %copy-start.4) | copy-done | bytes 924
  19.5 0.0 copy-start.5
  19.5 0.7 %copy-done.5 = s32[225]{0:T(256)S(1)} copy-done((s32[225]{0:T(256)S(1)}, s32[225]{0:T(256)}, u32[]{:S(2)}) %copy-start.5) | copy-done | bytes 924
  20.2 10.1 %remap.1 = (f32[2,6,8,3600]{3,2,1,0:T(8,128)}, f32[16,13,8,128]{3,2,1,0:T(8,128)S(1)}) custom-call(f32[2,14,8,3712]{3,2,1,0:T(8,128)S(1)} %get-tuple-element.7.full, f32[2,12,8,3712]{3,2,1,0:T(8,128)S(1)} %get-tuple-element.8.mid, f32[1,12,8,3712]{3,2,1,0:T(8,128)S(1)} %get-tuple-element.9.nxt, f32[12,12]{1,0:T(8,128)S(1)} %copy-done.3, s32[225]{0:T(256)S(1)} %bitcast.3, ...), custom_call_target="tpu_custom_call" | custom-call | flops 200000000 | bytes 18000000 | tf_op jit(solution)/shard_map/remap/pallas_call | solution.py:373
  30.4 17.8 %owner_sums.1 = f32[12,1024]{1,0:T(8,128)S(1)} custom-call(f32[2,2,4,13,8,128]{5,4,3,2,1,0:T(8,128)S(1)} %bitcast.2), custom_call_target="tpu_custom_call" | custom-call | flops 1000000 | bytes 4000000 | tf_op jit(solution)/shard_map/owner_sums/pallas_call | solution.py:466
  48.1 0.6 %copy.11 = f32[12,1024]{1,0:T(8,128)} copy(f32[12,1024]{1,0:T(8,128)S(1)} %owner_sums.1) | data formatting | bytes 98304
Async XLA Ops:
  0.6 1.4 %copy-start = (f32[2,6,8,3600]{3,2,1,0:T(8,128)S(1)}, f32[2,6,8,3600]{3,2,1,0:T(8,128)}, u32[]{:S(2)}) copy-start(f32[2,6,8,3600]{3,2,1,0:T(8,128)} %u_ref.1) | copy-start | bytes 4147204
  2.0 0.9 %copy-start.1 = (f32[8,3600]{1,0:T(8,128)S(1)}, f32[8,3600]{1,0:T(8,128)}, u32[]{:S(2)}) copy-start(f32[8,3600]{1,0:T(8,128)} %kap_ref.1) | copy-start | bytes 345604
  2.9 0.9 %copy-start.2 = (s32[8,3600]{1,0:T(8,128)S(1)}, s32[8,3600]{1,0:T(8,128)}, u32[]{:S(2)}) copy-start(s32[8,3600]{1,0:T(8,128)} %wet_ref.1) | copy-start | bytes 345604
  3.8 0.7 %copy-start.6 = (f32[6]{0:T(128)S(1)}, f32[6]{0:T(128)}, u32[]{:S(2)}) copy-start(f32[6]{0:T(128)} %kv_ref.1) | copy-start | bytes 76
  18.2 0.7 %copy-start.3 = (f32[12,12]{1,0:T(8,128)S(1)}, f32[12,12]{1,0:T(8,128)}, u32[]{:S(2)}) copy-start(f32[12,12]{1,0:T(8,128)} %coup_ref.1) | copy-start | bytes 1732
  18.9 0.7 %copy-start.4 = (s32[225,1]{0,1:T(1,128)S(1)}, s32[225,1]{0,1:T(1,128)}, u32[]{:S(2)}) copy-start(s32[225,1]{0,1:T(1,128)} %param.13) | copy-start | bytes 2704
  19.5 0.7 %copy-start.5 = (s32[225]{0:T(256)S(1)}, s32[225]{0:T(256)}, u32[]{:S(2)}) copy-start(s32[225]{0:T(256)} %tile_ref.1) | copy-start | bytes 2704

commit v5 on v4

--- a/solution.py
+++ b/solution.py
@@ -105,10 +105,15 @@
     return jnp.where(l < face[1], face[0], 0.0)
 
 
+GROUPS = (((0, 8), (8, 4), (12, 2)), ((0, 8), (8, 4)))
+N_GROUPS = sum(len(groups) for groups in GROUPS)
+
+
 def step_kernel(n, u_ref, kap_ref, wet_ref, kv_ref, full, mid, nxt, *refs):
-    outgoing, incoming, send, recv = refs
+    outgoing, incoming, (send, recv) = refs[:N_GROUPS], refs[N_GROUPS:2 * N_GROUPS], refs[2 * N_GROUPS:]
     me = lax.axis_index("blk")
-    incoming[...] = jnp.zeros_like(incoming)
+    for one in incoming:
+        one[...] = jnp.zeros_like(one)
     barrier = pltpu.get_barrier_semaphore()
     for other in (lax.rem(me + n - 1, n), lax.rem(me + 1, n)):
         pl.semaphore_signal(
@@ -130,17 +135,22 @@
         row = (0, ROWS - 1)[i]
         return slice(row, row + 1)
 
+    def grouped(far):
+        before = len(GROUPS[0]) * far
+        return [(before + k,) + group for k, group in enumerate(GROUPS[far])]
+
     def copies(far, i):
         return [pltpu.make_async_remote_copy(
-            src_ref=outgoing.at[far, i], dst_ref=incoming.at[far, i],
-            send_sem=send.at[far, i], recv_sem=recv.at[far, i],
+            src_ref=outgoing[k].at[i], dst_ref=incoming[k].at[i],
+            send_sem=send.at[2 * k + i], recv_sem=recv.at[2 * k + i],
             device_id={"blk": sides[i][1]}, device_id_type=pl.DeviceIdType.MESH,
-        )]
-
-    def start(far, source, rows):
+        ) for k, _, _ in grouped(far)]
+
+    def start(far, source):
         for i in range(2):
-            for q in range(rows):
-                outgoing[far, i, q:q + 1, :] = source[0, q, edge_row(i), :]
+            for k, first, number in grouped(far):
+                for q in range(number):
+                    outgoing[k][i, q:q + 1, :] = source[0, first + q, edge_row(i), :]
 
             @pl.when(sides[i][0])
             def _():
@@ -154,10 +164,11 @@
                 for one in copies(far, i):
                     one.wait_recv()
 
-    def spread_out(far, target, rows):
+    def spread_out(far, target):
         for i in range(2):
-            for q in range(rows):
-                target[1, q, edge_row(i), :] = incoming[far, i, q:q + 1, :]
+            for k, first, number in grouped(far):
+                for q in range(number):
+                    target[1, first + q, edge_row(i), :] = incoming[k][i, q:q + 1, :]
 
     def place(q, value):
         full[0, q, :, 0:cut] = value[:, 0:cut]
@@ -182,14 +193,13 @@
     place(12, kap_ref[...])
     place(13, wet_ref[...].astype(jnp.float32))
     full[1] = jnp.zeros(full.shape[1:], jnp.float32)
-    outgoing[...] = jnp.zeros_like(outgoing)
     pl.semaphore_wait(barrier, 2)
-    start(0, full, 14)
+    start(0, full)
     closed_step(full, full, mid, kv, lane, sub, tiles)
-    start(1, mid, 2 * NZ)
+    start(1, mid)
     mid[1] = jnp.zeros(mid.shape[1:], jnp.float32)
     arrive(0)
-    spread_out(0, full, 14)
+    spread_out(0, full)
 
     def near(t, carry):
         here = columns(t, tiles)[0]
@@ -204,7 +214,7 @@
     lax.fori_loop(0, tiles, near, 0)
     closed_step(mid, full, nxt, kv, lane, sub, tiles)
     arrive(1)
-    spread_out(1, mid, 2 * NZ)
+    spread_out(1, mid)
     for far in range(2):
         for i in range(2):
             @pl.when(sides[i][0])
@@ -226,8 +236,10 @@
         ),
         in_specs=[vmem] * 3 + [smem],
         out_specs=(vmem,) * 3,
-        scratch_shapes=[pltpu.VMEM((2, 2, 16, pad), jnp.float32)] * 2
-        + [pltpu.SemaphoreType.DMA((2, 2))] * 2,
+        scratch_shapes=[
+            pltpu.VMEM((2, number, pad), jnp.float32) for groups in GROUPS for _, number in groups
+        ] * 2
+        + [pltpu.SemaphoreType.DMA((2 * N_GROUPS,))] * 2,
         compiler_params=pltpu.CompilerParams(
             collective_id=1, has_side_effects=True, vmem_limit_bytes=24 * 2**20
         ),
@@ -328,7 +340,7 @@
             blocks[last * j + t] = value.astype(jnp.bfloat16)
         return carry
 
-    lax.fori_loop(1, last, align, 0, unroll=3)
+    lax.fori_loop(1, last, align, 0, unroll=9)
     for j in range(ROWS + 1):
         if j > 0:
             rows = pl.ds((j - 1) * WIDE, WIDE)
@@ -350,7 +362,7 @@
         acc[here, :] = acc[here, :] + value
         return carry
 
-    lax.fori_loop(0, count, product, 0, unroll=25)
+    lax.fori_loop(0, count, product, 0, unroll=45)
 
     owners = sums_ref.shape[0]
     quarter = owners // 4

time: 49 us -> 47 us (0.959)
  Pallas kernels: 41.6 us -> 39.5 us
    pallas_call x1, Pallas kernels: 17.8 us -> 16.5 us  [owner_part(): pl.pallas_call(functools.partial(owner_kernel, n), name='owner_sums', cos...]
    pallas_call x1, Pallas kernels: 10.1 us -> 9.21 us  [local_part(): pl.pallas_call(local_kernel, name='remap', cost_estimate=pl.CostEstimate(...]
where the time goes in v5:
time: 47 us; the launch traced here: 46.7 us
  Pallas kernels  39.5 us (84%)
  local copies, waits for them, and re-layouts  6.48 us (14%)
  between operations  0.68 us (1%)
    pallas_call x1, Pallas kernels, owner_part(): pl.pallas_call(functools.partial(owner_kernel, n), name='owner_sums', cos...  16.5 us
    pallas_call x1, Pallas kernels, step_part(): pl.pallas_call(functools.partial(step_kernel, n), name='two_steps', cost_...  13.8 us
    pallas_call x1, Pallas kernels, local_part(): pl.pallas_call(local_kernel, name='remap', cost_estimate=pl.CostEstimate(...  9.21 us
    unnamed x15, local copies, waits for them, and re-layouts  6.48 us

profile of v5, /device:TPU:0, one launch (start us, length us, event | category | flops | bytes accessed | tf_op | source)
XLA Modules:
  0.0 46.7 jit_solution(13669081859695963248)
XLA Ops:
  0.6 0.0 copy-start
  0.6 1.3 %copy-done = f32[2,6,8,3600]{3,2,1,0:T(8,128)S(1)} copy-done((f32[2,6,8,3600]{3,2,1,0:T(8,128)S(1)}, f32[2,6,8,3600]{3,2,1,0:T(8,128)}, u32[]{:S(2)}) %copy-start) | copy-done | bytes 1382424
  2.0 0.0 copy-start.1
  2.0 0.9 %copy-done.1 = f32[8,3600]{1,0:T(8,128)S(1)} copy-done((f32[8,3600]{1,0:T(8,128)S(1)}, f32[8,3600]{1,0:T(8,128)}, u32[]{:S(2)}) %copy-start.1) | copy-done | bytes 115224
  2.9 0.0 copy-start.2
  2.9 0.9 %copy-done.2 = s32[8,3600]{1,0:T(8,128)S(1)} copy-done((s32[8,3600]{1,0:T(8,128)S(1)}, s32[8,3600]{1,0:T(8,128)}, u32[]{:S(2)}) %copy-start.2) | copy-done | bytes 115224
  3.8 0.0 copy-start.6
  3.8 0.7 %copy-done.6 = f32[6]{0:T(128)S(1)} copy-done((f32[6]{0:T(128)S(1)}, f32[6]{0:T(128)}, u32[]{:S(2)}) %copy-start.6) | copy-done | bytes 48
  4.4 13.8 %two_steps.1 = (f32[2,14,8,3712]{3,2,1,0:T(8,128)S(1)}, f32[2,12,8,3712]{3,2,1,0:T(8,128)S(1)}, f32[1,12,8,3712]{3,2,1,0:T(8,128)S(1)}) custom-call(f32[2,6,8,3600]{3,2,1,0:T(8,128)S(1)} %copy-done, f32[8,3600]{1,0:T(8,128)S(1)} %copy-done.1, s32[8,3600]{1,0:T(8,128)S(1)} %copy-done.2, f32[6]{0:T(128)S(1)} %copy-done.6), custom_call_target="tpu_custom_call" | custom-call | flops 20000000 | bytes 12000000 | tf_op jit(solution)/shard_map/two_steps/pallas_call | solution.py:230
  18.3 0.0 copy-start.3
  18.3 0.7 %copy-done.3 = f32[12,12]{1,0:T(8,128)S(1)} copy-done((f32[12,12]{1,0:T(8,128)S(1)}, f32[12,12]{1,0:T(8,128)}, u32[]{:S(2)}) %copy-start.3) | copy-done | bytes 600
  19.0 0.0 copy-start.4
  19.0 0.7 %copy-done.4 = s32[225,1]{0,1:T(1,128)S(1)} copy-done((s32[225,1]{0,1:T(1,128)S(1)}, s32[225,1]{0,1:T(1,128)}, u32[]{:S(2)}) %copy-start.4) | copy-done | bytes 924
  19.7 0.0 copy-start.5
  19.7 0.7 %copy-done.5 = s32[225]{0:T(256)S(1)} copy-done((s32[225]{0:T(256)S(1)}, s32[225]{0:T(256)}, u32[]{:S(2)}) %copy-start.5) | copy-done | bytes 924
  20.4 9.2 %remap.1 = (f32[2,6,8,3600]{3,2,1,0:T(8,128)}, f32[16,13,8,128]{3,2,1,0:T(8,128)S(1)}) custom-call(f32[2,14,8,3712]{3,2,1,0:T(8,128)S(1)} %get-tuple-element.7.full, f32[2,12,8,3712]{3,2,1,0:T(8,128)S(1)} %get-tuple-element.8.mid, f32[1,12,8,3712]{3,2,1,0:T(8,128)S(1)} %get-tuple-element.9.nxt, f32[12,12]{1,0:T(8,128)S(1)} %copy-done.3, s32[225]{0:T(256)S(1)} %bitcast.3, ...), custom_call_target="tpu_custom_call" | custom-call | flops 200000000 | bytes 18000000 | tf_op jit(solution)/shard_map/remap/pallas_call | solution.py:385
  29.6 16.5 %owner_sums.1 = f32[12,1024]{1,0:T(8,128)S(1)} custom-call(f32[2,2,4,13,8,128]{5,4,3,2,1,0:T(8,128)S(1)} %bitcast.2), custom_call_target="tpu_custom_call" | custom-call | flops 1000000 | bytes 4000000 | tf_op jit(solution)/shard_map/owner_sums/pallas_call | solution.py:478
  46.1 0.6 %copy.11 = f32[12,1024]{1,0:T(8,128)} copy(f32[12,1024]{1,0:T(8,128)S(1)} %owner_sums.1) | data formatting | bytes 98304
Async XLA Ops:
  0.6 1.4 %copy-start = (f32[2,6,8,3600]{3,2,1,0:T(8,128)S(1)}, f32[2,6,8,3600]{3,2,1,0:T(8,128)}, u32[]{:S(2)}) copy-start(f32[2,6,8,3600]{3,2,1,0:T(8,128)} %u_ref.1) | copy-start | bytes 4147204
  2.0 0.9 %copy-start.1 = (f32[8,3600]{1,0:T(8,128)S(1)}, f32[8,3600]{1,0:T(8,128)}, u32[]{:S(2)}) copy-start(f32[8,3600]{1,0:T(8,128)} %kap_ref.1) | copy-start | bytes 345604
  2.9 0.9 %copy-start.2 = (s32[8,3600]{1,0:T(8,128)S(1)}, s32[8,3600]{1,0:T(8,128)}, u32[]{:S(2)}) copy-start(s32[8,3600]{1,0:T(8,128)} %wet_ref.1) | copy-start | bytes 345604
  3.8 0.7 %copy-start.6 = (f32[6]{0:T(128)S(1)}, f32[6]{0:T(128)}, u32[]{:S(2)}) copy-start(f32[6]{0:T(128)} %kv_ref.1) | copy-start | bytes 76
  18.3 0.7 %copy-start.3 = (f32[12,12]{1,0:T(8,128)S(1)}, f32[12,12]{1,0:T(8,128)}, u32[]{:S(2)}) copy-start(f32[12,12]{1,0:T(8,128)} %coup_ref.1) | copy-start | bytes 1732
  19.0 0.7 %copy-start.4 = (s32[225,1]{0,1:T(1,128)S(1)}, s32[225,1]{0,1:T(1,128)}, u32[]{:S(2)}) copy-start(s32[225,1]{0,1:T(1,128)} %param.13) | copy-start | bytes 2704
  19.7 0.7 %copy-start.5 = (s32[225]{0:T(256)S(1)}, s32[225]{0:T(256)}, u32[]{:S(2)}) copy-start(s32[225]{0:T(256)} %tile_ref.1) | copy-start | bytes 2704

commit v6 on v5

--- a/solution.py
+++ b/solution.py
@@ -247,7 +247,7 @@
 
 
 def local_kernel(
-    full, mid, nxt, coup_ref, dest_ref, tile_ref, w_hbm,
+    full, mid, nxt, coup_ref, seg_ref, w_hbm,
     next_ref, sums_ref,
     surf, blocks, acc, weights, w_sem,
 ):
@@ -357,7 +357,7 @@
 
     def product(g, carry):
         value = jnp.dot(blocks[g], weights[g], preferred_element_type=jnp.float32)
-        seg = dest_ref[g] * NTILE + tile_ref[g]
+        seg = seg_ref[g]
         here = pl.ds(pl.multiple_of(seg * WIDE, WIDE), WIDE)
         acc[here, :] = acc[here, :] + value
         return carry
@@ -377,7 +377,7 @@
     lax.fori_loop(0, owners, deliver, 0)
 
 
-def local_part(full, mid, nxt, coup, dest, tile, weights, length, owners):
+def local_part(full, mid, nxt, coup, seg, weights, length, owners):
     pad = full.shape[-1]
     count = weights.shape[0]
     vmem = pl.BlockSpec(memory_space=pltpu.VMEM)
@@ -390,7 +390,7 @@
             jax.ShapeDtypeStruct((2, NZ, ROWS, length), jnp.float32),
             jax.ShapeDtypeStruct((owners, FIELDS + 1, NTILE, AT), jnp.float32),
         ),
-        in_specs=[vmem] * 4 + [smem, smem, pl.BlockSpec(memory_space=pl.ANY)],
+        in_specs=[vmem] * 4 + [smem, pl.BlockSpec(memory_space=pl.ANY)],
         out_specs=(vmem, vmem),
         scratch_shapes=[
             pltpu.VMEM((ROWS * WIDE, pad), jnp.float32),
@@ -400,7 +400,7 @@
             pltpu.SemaphoreType.DMA,
         ],
         compiler_params=pltpu.CompilerParams(vmem_limit_bytes=44 * 2**20),
-    )(full, mid, nxt, coup, dest, tile, weights)
+    )(full, mid, nxt, coup, seg, weights)
 
 
 PARTS = ((0, 4), (4, 7), (7, 10), (10, 13))
@@ -504,7 +504,7 @@
     size = lax.axis_size("blk")
     steps = step_part(ocean_state, kappa_h, wet_depth, kappa_v, size)
     ocean_next, sums = local_part(
-        *steps, coupling, dest_of_block.reshape(-1), tile_of_block, remap_weights,
+        *steps, coupling, dest_of_block.reshape(-1) * NTILE + tile_of_block, remap_weights,
         ocean_state.shape[-1], size,
     )
     return ocean_next, owner_part(sums)

time: 47 us -> 47 us (level)
  other arithmetic: 0 us -> 1.36 us
  local copies, waits for them, and re-layouts: 6.48 us -> 5.13 us
    unnamed x15 -> x11, local copies, waits for them, and re-layouts: 6.48 us -> 5.13 us
    mul x0 -> x1, other arithmetic: none -> 0.68 us  [body(): dest_of_block.reshape(-1) * NTILE + tile_of_block]
    add x0 -> x1, other arithmetic: none -> 0.68 us  [body(): dest_of_block.reshape(-1) * NTILE + tile_of_block]
where the time goes in v6:
time: 47 us; the launch traced here: 46.7 us
  Pallas kernels  39.5 us (84%)
  local copies, waits for them, and re-layouts  5.13 us (11%)
  other arithmetic  1.36 us (3%)
  between operations  0.67 us (1%)
    pallas_call x1, Pallas kernels, owner_part(): pl.pallas_call(functools.partial(owner_kernel, n), name='owner_sums', cos...  16.5 us
    pallas_call x1, Pallas kernels, step_part(): pl.pallas_call(functools.partial(step_kernel, n), name='two_steps', cost_...  13.8 us
    pallas_call x1, Pallas kernels, local_part(): pl.pallas_call(local_kernel, name='remap', cost_estimate=pl.CostEstimate(...  9.2 us
    unnamed x11, local copies, waits for them, and re-layouts  5.13 us

profile of v6, /device:TPU:0, one launch (start us, length us, event | category | flops | bytes accessed | tf_op | source)
XLA Modules:
  0.0 46.7 jit_solution(13111412009257826992)
XLA Ops:
  0.6 0.7 %broadcast_multiply_fusion = s32[225,1]{0,1:T(1,128)S(1)} fusion(s32[225,1]{0,1:T(1,128)} %param.13), kind=kLoop, calls=%fused_computation | loop fusion | flops 225 | bytes 1800 | tf_op jit(solution)/shard_map/mul | solution.py:507
  1.3 0.7 %add.3.seg_ref = s32[225]{0:T(256)S(1)} add(s32[225]{0:T(256)S(1)} %bitcast.3, s32[225]{0:T(256)} %param.14) | non-fusion elementwise | flops 225 | bytes 2700 | tf_op jit(solution)/shard_map/add | solution.py:507
  2.0 0.0 copy-start
  2.0 1.4 %copy-done = f32[2,6,8,3600]{3,2,1,0:T(8,128)S(1)} copy-done((f32[2,6,8,3600]{3,2,1,0:T(8,128)S(1)}, f32[2,6,8,3600]{3,2,1,0:T(8,128)}, u32[]{:S(2)}) %copy-start) | copy-done | bytes 1382424
  3.4 0.0 copy-start.1
  3.4 0.9 %copy-done.1 = f32[8,3600]{1,0:T(8,128)S(1)} copy-done((f32[8,3600]{1,0:T(8,128)S(1)}, f32[8,3600]{1,0:T(8,128)}, u32[]{:S(2)}) %copy-start.1) | copy-done | bytes 115224
  4.3 0.0 copy-start.2
  4.3 0.9 %copy-done.2 = s32[8,3600]{1,0:T(8,128)S(1)} copy-done((s32[8,3600]{1,0:T(8,128)S(1)}, s32[8,3600]{1,0:T(8,128)}, u32[]{:S(2)}) %copy-start.2) | copy-done | bytes 115224
  5.2 0.0 copy-start.4
  5.2 0.7 %copy-done.4 = f32[6]{0:T(128)S(1)} copy-done((f32[6]{0:T(128)S(1)}, f32[6]{0:T(128)}, u32[]{:S(2)}) %copy-start.4) | copy-done | bytes 48
  5.8 13.8 %two_steps.1 = (f32[2,14,8,3712]{3,2,1,0:T(8,128)S(1)}, f32[2,12,8,3712]{3,2,1,0:T(8,128)S(1)}, f32[1,12,8,3712]{3,2,1,0:T(8,128)S(1)}) custom-call(f32[2,6,8,3600]{3,2,1,0:T(8,128)S(1)} %copy-done, f32[8,3600]{1,0:T(8,128)S(1)} %copy-done.1, s32[8,3600]{1,0:T(8,128)S(1)} %copy-done.2, f32[6]{0:T(128)S(1)} %copy-done.4), custom_call_target="tpu_custom_call" | custom-call | flops 20000000 | bytes 12000000 | tf_op jit(solution)/shard_map/two_steps/pallas_call | solution.py:230
  19.7 0.0 copy-start.3
  19.7 0.7 %copy-done.3 = f32[12,12]{1,0:T(8,128)S(1)} copy-done((f32[12,12]{1,0:T(8,128)S(1)}, f32[12,12]{1,0:T(8,128)}, u32[]{:S(2)}) %copy-start.3) | copy-done | bytes 600
  20.4 9.2 %remap.1 = (f32[2,6,8,3600]{3,2,1,0:T(8,128)}, f32[16,13,8,128]{3,2,1,0:T(8,128)S(1)}) custom-call(f32[2,14,8,3712]{3,2,1,0:T(8,128)S(1)} %get-tuple-element.7.full, f32[2,12,8,3712]{3,2,1,0:T(8,128)S(1)} %get-tuple-element.8.mid, f32[1,12,8,3712]{3,2,1,0:T(8,128)S(1)} %get-tuple-element.9.nxt, f32[12,12]{1,0:T(8,128)S(1)} %copy-done.3, s32[225]{0:T(256)S(1)} %add.3.seg_ref, ...), custom_call_target="tpu_custom_call" | custom-call | flops 200000000 | bytes 18000000 | tf_op jit(solution)/shard_map/remap/pallas_call | solution.py:385
  29.6 16.5 %owner_sums.1 = f32[12,1024]{1,0:T(8,128)S(1)} custom-call(f32[2,2,4,13,8,128]{5,4,3,2,1,0:T(8,128)S(1)} %bitcast.2), custom_call_target="tpu_custom_call" | custom-call | flops 1000000 | bytes 4000000 | tf_op jit(solution)/shard_map/owner_sums/pallas_call | solution.py:478
  46.1 0.6 %copy.11 = f32[12,1024]{1,0:T(8,128)} copy(f32[12,1024]{1,0:T(8,128)S(1)} %owner_sums.1) | data formatting | bytes 98304
Async XLA Ops:
  2.0 1.4 %copy-start = (f32[2,6,8,3600]{3,2,1,0:T(8,128)S(1)}, f32[2,6,8,3600]{3,2,1,0:T(8,128)}, u32[]{:S(2)}) copy-start(f32[2,6,8,3600]{3,2,1,0:T(8,128)} %u_ref.1) | copy-start | bytes 4147204
  3.4 0.9 %copy-start.1 = (f32[8,3600]{1,0:T(8,128)S(1)}, f32[8,3600]{1,0:T(8,128)}, u32[]{:S(2)}) copy-start(f32[8,3600]{1,0:T(8,128)} %kap_ref.1) | copy-start | bytes 345604
  4.3 0.9 %copy-start.2 = (s32[8,3600]{1,0:T(8,128)S(1)}, s32[8,3600]{1,0:T(8,128)}, u32[]{:S(2)}) copy-start(s32[8,3600]{1,0:T(8,128)} %wet_ref.1) | copy-start | bytes 345604
  5.2 0.7 %copy-start.4 = (f32[6]{0:T(128)S(1)}, f32[6]{0:T(128)}, u32[]{:S(2)}) copy-start(f32[6]{0:T(128)} %kv_ref.1) | copy-start | bytes 76
  19.7 0.7 %copy-start.3 = (f32[12,12]{1,0:T(8,128)S(1)}, f32[12,12]{1,0:T(8,128)}, u32[]{:S(2)}) copy-start(f32[12,12]{1,0:T(8,128)} %coup_ref.1) | copy-start | bytes 1732
